TPU v7x, 128 devices: a whole 4x4x4 slice. The times are simulated.
128 devices in a mesh: proj: 32 (over z, x, core), det: 4 (over y).
Axes of the slice: x: 4, y: 4, z: 4, core: 2. Of those that a mesh axis runs over, the one named last changes fastest.
Arguments:
- raw_frames: bfloat16 [2048, 64, 2048], P('proj', None, 'det'), may hold values from 0.25 to 2.125
- slot_angle: int32 [2048], replicated, may hold values from 0 to 1024, as said below
- segment_of: int32 [1024], replicated, may hold values from 0 to 7, never falling along the last dimension, each value on 1 to 256 neighbouring positions
- seg_owner: int32 [8], replicated, may hold values from 0 to 31
- flat_stack: float32 [256, 64, 2048], P('proj', None, 'det'), may hold values from 1 to 2
- dark_stack: float32 [256, 64, 2048], P('proj', None, 'det'), may hold values from 0 to 0.2
- row_order: int32 [64], replicated, may hold values from 0 to 63, each once
- bin_counts: int32 [64], replicated, may hold values from 2 to 5
Outputs:
- codes: float32 [1024, 64, 2048], P(None, 'proj', 'det')
Inputs may be any that keep to these rules, and one draw needn't show every extreme that they name: `slot_angle`: index p of proj holds slots 64 * p to 64 * p + 63. Every angle 0 to 1023 stands in exactly one slot; a device's filled slots come first and its other slots hold 1024. Indices 2k and 2k + 1 of proj together fill exactly 64 slots, and some index fills all 64. `segment_of`: never falls from one angle to the next; every segment has an angle. `seg_owner`: each value is an index of proj. `row_order`: A permutation of the rows.
All inputs are finite; a program needn't handle non-finite values.
Results may differ from a plain program's by a relative error of at most 0.0029.
Values may be sent and summed in bfloat16 or wider, within the bound.
A program may use at most 128 MiB of HBM per device.

v0:
```python
import jax
import jax.numpy as jnp
from jax import lax
from jax.sharding import PartitionSpec as P

RIM = 8


epsilon = 1e-06


def broadcast(x, axis, root):
    mine = lax.axis_index(axis) == root
    return lax.psum(jnp.where(mine, x, jnp.zeros_like(x)), axis)


def padded_2(block, sides, width):
    for axis, dim in sides:
        count = lax.axis_size(axis)
        forward = [(i, i + 1) for i in range(count - 1)]
        backward = [(target, source) for source, target in forward]
        low = lax.ppermute(
            lax.slice_in_dim(block, block.shape[dim] - width, None, axis=dim), axis, forward
        )
        high = lax.ppermute(lax.slice_in_dim(block, 0, width, axis=dim), axis, backward)
        block = jnp.concatenate([low, block, high], axis=dim)
    return block


def negative_log(frames, segment, flat_fields, dark_fields):
    flat_rows = jnp.take(flat_fields, segment, axis=0)
    dark_rows = jnp.take(dark_fields, segment, axis=0)
    ratio = (frames.astype(jnp.float32) - dark_rows) / (flat_rows - dark_rows)
    return (-jnp.log(ratio)).astype(jnp.bfloat16)


def gather_fields(flat_stack, dark_stack, seg_owner):
    segments = seg_owner.shape[0]
    flat_list = []
    dark_list = []
    for segment in range(segments):
        flat_one, dark_one = (
            broadcast(flat_stack[segment], "proj", seg_owner[segment]),
            broadcast(dark_stack[segment], "proj", seg_owner[segment]),
        )
        flat_list.append(flat_one)
        dark_list.append(dark_one)
    return (jnp.stack(flat_list), jnp.stack(dark_list))


def place_by_angle(received, arrival, total_angles):
    locate = (
        jnp.zeros((total_angles,), jnp.int32)
        .at[arrival]
        .set(jnp.arange(arrival.shape[0], dtype=jnp.int32), mode="drop")
    )
    return received[locate]


def on_device(
    raw_frames, slot_angle, segment_of, seg_owner, flat_stack, dark_stack, row_order, bin_counts
):
    proj_index = lax.axis_index("proj")
    proj_count = lax.axis_size("proj")
    total_angles = segment_of.shape[0]
    slots = raw_frames.shape[0]
    slab = raw_frames.shape[1] // proj_count
    my_angles = lax.dynamic_slice_in_dim(slot_angle, proj_index * slots, slots)
    flat_fields, dark_fields = gather_fields(flat_stack, dark_stack, seg_owner)
    segment = segment_of[jnp.minimum(my_angles, total_angles - 1)]
    values = negative_log(raw_frames, segment, flat_fields, dark_fields)
    ordered = values[:, row_order, :]
    received = lax.all_to_all(ordered, "proj", split_axis=1, concat_axis=0, tiled=True)
    sinogram = place_by_angle(received, slot_angle, total_angles)
    profile = jnp.sum(sinogram, axis=0, dtype=jnp.float32) / total_angles
    padded = padded_2(profile, (("det", 1),), RIM)
    cols_dev = profile.shape[1]
    window_sum = padded[:, 0:cols_dev]
    for shifted in range(1, 2 * RIM + 1):
        window_sum = window_sum + padded[:, shifted : shifted + cols_dev]
    total_cols = cols_dev * lax.axis_size("det")
    column = lax.axis_index("det") * cols_dev + jnp.arange(cols_dev, dtype=jnp.int32)
    counted = (jnp.minimum(column + RIM, total_cols - 1) - jnp.maximum(column - RIM, 0) + 1).astype(
        jnp.float32
    )
    smooth = window_sum / counted
    corrected = sinogram.astype(jnp.float32) - (profile - smooth)[None]
    magnitude = lax.psum(jnp.sum(jnp.abs(corrected), axis=(0, 2)), "det")
    scale = magnitude / (total_angles * total_cols) + epsilon
    my_rows = lax.dynamic_slice_in_dim(row_order, proj_index * slab, slab)
    factor = bin_counts[my_rows].astype(jnp.float32) / scale
    return corrected * factor[None, :, None]


def solution(mesh):
    return jax.shard_map(
        on_device,
        mesh=mesh,
        in_specs=(
            P("proj", None, "det"),
            P(),
            P(),
            P(),
            P("proj", None, "det"),
            P("proj", None, "det"),
            P(),
            P(),
        ),
        out_specs=P(None, "proj", "det"),
        check_vma=False,
    )
```

profile of v0, /device:TPU:0, one launch (start us, length us, event | category | flops | bytes accessed | tf_op | source)
XLA Modules:
  0.0 296.4 jit_solution(13011449313521776021)
XLA Ops:
  6.6 1.6 fusion.41
  13.2 2.3 slice_select_fusion.8
  15.5 2.3 slice_select_fusion
  18.6 8.0 %scatter_custom_fusion = s32[1024]{0:T(1024)S(1)} fusion(s32[2048]{0:T(1024)S(1)} %compare_select_fusion, s32[2048]{0:T(1024)S(1)} %iota.8, s32[]{:T(128)} %constant.30.clone.1), kind=kCustom, calls=%fused_computation.118 | custom fusion | bytes 4100 | tf_op jit(solution)/shard_map/scatter | solution.py:55
  26.8 105.1 %all-reduce.3.cloned.1.call-done = (f32[1,64,512]{2,1,0:T(8,128)}, f32[1,64,512]{2,1,0:T(8,128)}, f32[1,64,512]{2,1,0:T(8,128)}, f32[1,64,512]{2,1,0:T(8,128)}, ...) async-done(((f32[1,64,512]{2,1,0:T(8,128)}, ...) | async-done | bytes 2097168 | tf_op jit(solution)/shard_map/psum | solution.py:14
  133.7 0.9 constant_dynamic-update-slice_fusion.14
  134.6 0.9 constant_dynamic-update-slice_fusion.13
  135.5 0.9 constant_dynamic-update-slice_fusion.12
  136.4 0.9 constant_dynamic-update-slice_fusion.11
  137.3 0.9 constant_dynamic-update-slice_fusion.10
  138.2 0.9 constant_dynamic-update-slice_fusion.9
  139.2 0.9 constant_dynamic-update-slice_fusion.6
  140.1 0.9 constant_dynamic-update-slice_fusion.5
  141.0 0.9 constant_dynamic-update-slice_fusion.4
  144.7 1.0 constant_dynamic-update-slice_fusion
  145.7 4.3 %gather_fusion.4 = f32[64,64,512]{2,1,0:T(8,128)} fusion(f32[8,64,512]{2,1,0:T(8,128)S(1)} %get-tuple-element.48, s32[1024]{0:T(1024)S(1)} %pad_clamp_fusion.2), kind=kCustom, calls=%fused_computation.clone | custom fusion | bytes 16777472 | tf_op jit(solution)/shard_map/jit(_take)/gather | solution.py:32
  150.0 4.3 %gather_fusion.5 = f32[64,64,512]{2,1,0:T(8,128)} fusion(f32[8,64,512]{2,1,0:T(8,128)S(1)} %get-tuple-element.49, s32[1024]{0:T(1024)S(1)} %pad_clamp_fusion.2), kind=kCustom, calls=%fused_computation.1.clone | custom fusion | bytes 16777472 | tf_op jit(solution)/shard_map/jit(_take)/gather | solution.py:31
  154.3 8.6 %fusion.3 = bf16[64,64,512]{2,1,0:T(8,128)(2,1)S(1)} fusion(f32[64,64,512]{2,1,0:T(8,128)} %gather_fusion.5, f32[64,64,512]{2,1,0:T(8,128)} %gather_fusion.4, bf16[64,64,512]{2,1,0:T(8,128)(2,1)} %param.10, pred[64]{0:T(512)(128)(4,1)S(1)} %compare_and_fusion), kind=kLoop, calls=%fused_computation.11 | loop fusion | flops 16777216 | bytes 25165888 | tf_op jit(solution)/shard_map/convert_element_type | solution.py:34
  162.9 4.4 %copy.12 = bf16[64,64,512]{2,0,1:T(8,128)(2,1)} copy(bf16[64,64,512]{2,1,0:T(8,128)(2,1)S(1)} %fusion.3) | data formatting | bytes 8388608 | tf_op jit(solution)/shard_map/convert_element_type | solution.py:34
  167.3 5.0 %gather_fusion.1 = bf16[64,64,512]{2,1,0:T(8,128)(2,1)} fusion(bf16[64,64,512]{2,0,1:T(8,128)(2,1)} %copy.12, s32[1024]{0:T(1024)S(1)} %get-tuple-element.51), kind=kCustom, calls=%fused_computation.3 | custom fusion | bytes 8388864 | tf_op jit(solution)/shard_map/gather | solution.py:72
  172.2 5.4 %all-to-all-start = ((bf16[64,64,512]{2,0,1:T(8,128)(2,1)}), bf16[64,64,512]{2,0,1:T(8,128)(2,1)}, u32[]{:S(2)}, u32[]{:S(2)}) async-start(bf16[64,64,512]{2,0,1:T(8,128)(2,1)} %bitcast.13), calls=%async_computation | async-start | bytes 8388608 | tf_op jit(solution)/shard_map/all_to_all | solution.py:73
  177.8 53.2 %all-to-all-done = bf16[64,64,512]{2,0,1:T(8,128)(2,1)} async-done(((bf16[64,64,512]{2,0,1:T(8,128)(2,1)}), bf16[64,64,512]{2,0,1:T(8,128)(2,1)}, u32[]{:S(2)}, u32[]{:S(2)}) %all-to-all-start) | async-done | bytes 4194336 | tf_op jit(solution)/shard_map/all_to_all | solution.py:73
  231.0 2.7 copy.13
  233.6 19.0 %copy.14 = bf16[2048,2,512]{2,1,0:T(2,128)(2,1)} copy(bf16[2048,2,512]{2,0,1:T(8,128)(2,1)S(1)} %bitcast.14) | data formatting | bytes 8388608 | tf_op jit(solution)/shard_map/all_to_all | solution.py:73
  252.7 8.1 %gather_fusion.2 = bf16[1024,2,512]{2,1,0:T(2,128)(2,1)S(1)} fusion(bf16[2048,2,512]{2,1,0:T(2,128)(2,1)} %copy.14, s32[1024]{0:T(1024)S(1)} %get-tuple-element.50), kind=kCustom, calls=%fused_computation.4 | custom fusion | bytes 4198400 | tf_op jit(solution)/shard_map/gather | solution.py:57
  260.8 1.8 convert_reduce_fusion
  262.6 3.4 %collective-permute-start = (f32[2,8]{1,0:T(2,128)S(1)}, f32[2,8]{1,0:T(2,128)S(1)}, u32[]{:S(2)}, u32[]{:S(2)}) collective-permute-start(f32[2,8]{1,0:T(2,128)S(1)} %get-tuple-element.38), channel_id=1, source_target_pairs={{0,1},{1,2},{2,3},{4,5},{5,6},{6,7},{8,9},{9,10},{10,11},{12,13},{... | collective-permute-start | bytes 200 | tf_op jit(solution)/shard_map/ppermute | solution.py:22
  266.0 1.3 collective-permute-start.1
  267.3 4.2 %collective-permute-done.1 = f32[2,8]{1,0:T(2,128)S(1)} collective-permute-done((f32[2,8]{1,0:T(2,128)S(1)}, f32[2,8]{1,0:T(2,128)S(1)}, u32[]{:S(2)}, u32[]{:S(2)}) %collective-permute-start.1) | collective-permute-done | bytes 96 | tf_op jit(solution)/shard_map/ppermute | solution.py:25
  271.6 4.4 %fusion.6 = f32[2]{0:T(128)S(1)} fusion(bf16[1024,2,512]{2,1,0:T(2,128)(2,1)S(1)} %gather_fusion.2, f32[2,512]{1,0:T(2,128)S(1)} %divide_subtract_fusion), kind=kLoop, calls=%fused_computation.16 | loop fusion | flops 4194302 | bytes 2101256 | tf_op jit(solution)/shard_map/reduce_sum | solution.py:88
  276.7 9.2 %psum.135 = f32[2]{0:T(128)S(1)} all-reduce(f32[2]{0:T(128)S(1)} %fusion.6), channel_id=1, replica_groups=mesh['proj'=32,'det'=4] {'det'}, use_global_device_ids=true, to_apply=%region_19.21 | all-reduce | flops 2 | bytes 16 | tf_op jit(solution)/shard_map/psum | solution.py:88
  285.9 3.7 %fusion.4 = f32[1024,2,512]{2,1,0:T(2,128)} fusion(bf16[1024,2,512]{2,1,0:T(2,128)(2,1)S(1)} %gather_fusion.2, f32[2]{0:T(128)S(1)} %add_divide_fusion, f32[2,512]{1,0:T(2,128)S(1)} %divide_subtract_fusion), kind=kLoop, calls=%fused_computation.14 | loop fusion | flops 3145728 | bytes 6295560 | tf_op jit(solution)/shard_map/mul | solution.py:92
  (34 shorter events, 6.4 us)
Async XLA Ops:
  6.5 11.4 %copy-start = (s32[1024]{0:T(1024)S(1)}, s32[1024]{0:T(1024)}, u32[]{:S(2)}) copy-start(s32[1024]{0:T(1024)} %param.12) | copy-start | bytes 12292
  6.5 11.3 %copy-start.2 = (s32[2048]{0:T(1024)S(1)}, s32[2048]{0:T(1024)}, u32[]{:S(2)}) copy-start(s32[2048]{0:T(1024)} %param.11) | copy-start | bytes 24580
  6.5 20.2 %copy-start.3 = (s32[64]{0:T(128)S(1)}, s32[64]{0:T(128)}, u32[]{:S(2)}) copy-start(s32[64]{0:T(128)} %param.16) | copy-start | bytes 772
  6.5 125.3 %all-reduce.3.cloned.1.call-start = ((), (), s32[]{:S(2)}) async-start(), calls=%async_computation.1 | async-start | bytes 4194304 | tf_op jit(solution)/shard_map/psum | solution.py:14
  172.2 58.7 %all-to-all-start = ((bf16[64,64,512]{2,0,1:T(8,128)(2,1)}), bf16[64,64,512]{2,0,1:T(8,128)(2,1)}, u32[]{:S(2)}, u32[]{:S(2)}) async-start(bf16[64,64,512]{2,0,1:T(8,128)(2,1)} %bitcast.13), calls=%async_computation | async-start | bytes 8388608 | tf_op jit(solution)/shard_map/all_to_all | solution.py:73
  252.7 23.4 %copy-start.1 = (s32[64]{0:T(128)S(1)}, s32[64]{0:T(128)}, u32[]{:S(2)}) copy-start(s32[64]{0:T(128)} %param.17) | copy-start | bytes 772
  262.6 4.7 %collective-permute-start = (f32[2,8]{1,0:T(2,128)S(1)}, f32[2,8]{1,0:T(2,128)S(1)}, u32[]{:S(2)}, u32[]{:S(2)}) collective-permute-start(f32[2,8]{1,0:T(2,128)S(1)} %get-tuple-element.38), channel_id=1, source_target_pairs={{0,1},{1,2},{2,3},{4,5},{5,6},{6,7},{8,9},{9,10},{10,11},{12,13},{... | collective-permute-start | bytes 200 | tf_op jit(solution)/shard_map/ppermute | solution.py:22
  266.0 5.5 %collective-permute-start.1 = (f32[2,8]{1,0:T(2,128)S(1)}, f32[2,8]{1,0:T(2,128)S(1)}, u32[]{:S(2)}, u32[]{:S(2)}) collective-permute-start(f32[2,8]{1,0:T(2,128)S(1)} %get-tuple-element.39), channel_id=1, source_target_pairs={{1,0},{2,1},{3,2},{5,4},{6,5},{7,6},{9,8},{10,9},{11,10},{13,12},{... | collective-permute-start | bytes 200 | tf_op jit(solution)/shard_map/ppermute | solution.py:25
Sparse Core Ops, SparseCore 0:
  17.9 113.8 all-reduce.2
where the time goes:
time: 297 us; the launch traced here: 296 us
  waiting for transfers between devices  162 us (55%)
  local copies, waits for them, and re-layouts  72.7 us (24%)
  other arithmetic  23.4 us (8%)
  between operations  18.6 us (6%)
  starting transfers between devices  10.1 us (3%)
  blocking collectives  9.19 us (3%)
    psum x1, waiting for transfers between devices, broadcast(): return lax.psum(jnp.where(mine, x, jnp.zeros_like(x)), axis)  105 us
    all_to_all x1, waiting for transfers between devices, on_device(): lax.all_to_all(ordered, 'proj', split_axis=1, concat_axis=0, tiled=True)  53.2 us
    all_to_all x2, local copies, waits for them, and re-layouts, on_device(): lax.all_to_all(ordered, 'proj', split_axis=1, concat_axis=0, tiled=True)  21.7 us
    unnamed x22, local copies, waits for them, and re-layouts  12.8 us
    psum x1, blocking collectives, on_device(): magnitude = lax.psum(jnp.sum(jnp.abs(corrected), axis=(0, 2)), 'det')  9.19 us
    convert_element_type x1, other arithmetic, negative_log(): return (-jnp.log(ratio)).astype(jnp.bfloat16)  8.59 us
    gather x1, local copies, waits for them, and re-layouts, place_by_angle(): return received[locate]  8.07 us
    scatter x1, local copies, waits for them, and re-layouts, place_by_angle(): locate = jnp.zeros((total_angles,), jnp.int32).at[arrival].set(jnp.arange...  8.04 us
  transfers between devices with their start and end apart: 4, of which 3 were waited for; matrix products, arithmetic and copies ran while one was open for 3% of the time, Pallas kernels for 0%

commit v1 on v0

v1 whole, which is shorter than its diff:
```python
import functools

import jax
import jax.numpy as jnp
from jax import lax
from jax.experimental import pallas as pl
from jax.experimental.pallas import tpu as pltpu
from jax.sharding import PartitionSpec as P

MESH = pl.DeviceIdType.MESH

SLOTS = 64
HALF = 32
ANGLES = 1024
ROWS = 64
COLS_DEV = 512
COLS = 2048
SEGS = 8
RIM = 8
PROJ = 32
CHIPS = 16
DET = 4
TILES = COLS_DEV // 128
PARTS = 4
FRAMES = HALF // PARTS
PAIRS = FRAMES // 2
EPSILON = 1e-6
DARK_STEP = 0.2 / 65535.0
FLAT_STEP = 1.0 / 65535.0


def stack_tiles(frame):
    return jnp.concatenate([frame[:, 128 * t : 128 * (t + 1)] for t in range(TILES)], axis=0)


def coded(field, low, step):
    q = jnp.floor((field - low) * (1.0 / step) + 0.5)
    q = jnp.clip(q, 0.0, 65535.0)
    high = jnp.floor(q * (1.0 / 256.0))
    return high.astype(jnp.bfloat16), (q - 256.0 * high).astype(jnp.bfloat16)


def exchange(
    slot_angle,
    segment_of,
    seg_owner,
    row_order,
    bin_counts,
    raw,
    flat,
    dark,
    y_out,
    delta_out,
    factor_out,
    where_out,
    own,
    other,
    send,
    recv,
    flat_v,
    dark_v,
    pick_f,
    pick,
    fsend,
    fpart,
    fjoin,
    frecv,
    dark_s,
    logflat_s,
    profs,
    sums,
    load_sem,
    field_sem,
    swap_ssem,
    swap_rsem,
    send_sem,
    recv_sem,
    fswap_sem,
    fsend_sem,
    frecv_sem,
    small_ssem,
    small_rsem,
):
    proj = lax.axis_index("proj")
    det = lax.axis_index("det")
    core = proj % 2
    chip = proj // 2
    col = chip % 4
    lay = chip // 4
    mate = proj + 1 - 2 * core

    def away(t):
        c = (core + t) % 2
        x = (col + t // 2) % 4
        z = (lay + t // 8) % 4
        return (z * 4 + x) * 2 + c

    def back(t):
        c = (core + t) % 2
        x = (col + 4 - (t // 2) % 4) % 4
        z = (lay + 4 - t // 8) % 4
        return (z * 4 + x) * 2 + c

    loads = []
    for part in range(PARTS):
        copy = pltpu.make_async_copy(
            raw.at[pl.ds(FRAMES * part, FRAMES)],
            own.at[pl.ds(FRAMES * part, FRAMES)],
            load_sem.at[part],
        )
        copy.start()
        loads.append(copy)
    flat_copy = pltpu.make_async_copy(flat, flat_v, field_sem.at[0])
    dark_copy = pltpu.make_async_copy(dark, dark_v, field_sem.at[1])
    flat_copy.start()
    dark_copy.start()

    barrier = pltpu.get_barrier_semaphore()

    @pl.loop(1, PROJ)
    def _(t):
        pl.semaphore_signal(
            barrier, inc=1, device_id=(away(t), det), device_id_type=MESH
        )

    for t in range(1, DET):
        pl.semaphore_signal(
            barrier, inc=1, device_id=(proj, (det + t) % DET), device_id_type=MESH
        )

    sub = lax.broadcasted_iota(jnp.int32, (8, 256), 0)
    lane = lax.broadcasted_iota(jnp.int32, (8, 256), 1)

    @pl.loop(0, PROJ)
    def _(i):
        p = 2 * (i % CHIPS) + i // CHIPS
        row = jnp.where(sub % 2 == 0, row_order[2 * p], row_order[2 * p + 1])
        hit = lane == row + (sub // 2) * ROWS
        pick_f[pl.ds(pl.multiple_of(8 * i, 8), 8), :] = jnp.where(hit, 1.0, 0.0)

    pick[...] = pick_f[...].astype(jnp.bfloat16)

    pl.semaphore_wait(barrier, PROJ - 1 + DET - 1)

    swaps = []
    for part in range(PARTS):
        first = HALF - FRAMES * (part + 1)
        copy = pltpu.make_async_remote_copy(
            src_ref=raw.at[pl.ds(HALF + first, FRAMES)],
            dst_ref=other.at[pl.ds(first, FRAMES)],
            send_sem=swap_ssem.at[part],
            recv_sem=swap_rsem.at[part],
            device_id=(mate, det),
            device_id_type=MESH,
        )
        copy.start()
        swaps.append(copy)

    def frame_copy(part, t, target, slot):
        return pltpu.make_async_remote_copy(
            src_ref=send.at[part, slot],
            dst_ref=recv.at[part, proj],
            send_sem=send_sem.at[part, t],
            recv_sem=recv_sem.at[part, proj],
            device_id=(target, det),
            device_id_type=MESH,
        )

    def slot_of(p):
        return (p % 2) * CHIPS + p // 2

    def ship_frames(part):
        loads[part].wait()
        swaps[part].wait_recv()

        @pl.loop(0, PAIRS)
        def _(j):
            merged = []
            for f in range(2):
                k = FRAMES * part + 2 * j + f
                filled = slot_angle[SLOTS * proj + k] < ANGLES
                merged.append(stack_tiles(jnp.where(filled, own[k], other[HALF - 1 - k])))
            moved = jnp.dot(
                pick[...], jnp.concatenate(merged, axis=1), preferred_element_type=jnp.float32
            ).reshape(PROJ, 8, 256)
            pair = jnp.concatenate([moved[:, :, :128], moved[:, :, 128:]], axis=1)
            send[part, :, j] = pair.astype(jnp.bfloat16)

        @pl.loop(1, PROJ)
        def _(t):
            target = away(t)
            frame_copy(part, t, target, slot_of(target)).start()

        recv[part, proj] = send[part, slot_of(proj)]

    def join_copy():
        return pltpu.make_async_remote_copy(
            src_ref=fsend.at[pl.ds((1 - core) * CHIPS, CHIPS)],
            dst_ref=fpart,
            send_sem=fswap_sem.at[0],
            recv_sem=fswap_sem.at[1],
            device_id=(mate, det),
            device_id_type=MESH,
        )

    def field_copy(t, target_chip):
        return pltpu.make_async_remote_copy(
            src_ref=fjoin.at[target_chip],
            dst_ref=frecv.at[chip],
            send_sem=fsend_sem.at[t],
            recv_sem=frecv_sem.at[chip],
            device_id=(2 * target_chip + core, det),
            device_id_type=MESH,
        )

    def code_fields():
        flat_copy.wait()
        dark_copy.wait()

        @pl.loop(0, SEGS)
        def _(s):
            mine = jnp.where(seg_owner[s] == proj, 1.0, 0.0)
            moved = []
            for ref, low, step in ((flat_v, 1.0, FLAT_STEP), (dark_v, 0.0, DARK_STEP)):
                high, small = coded(stack_tiles(ref[s]), low, step)
                both = jnp.dot(
                    pick[...], jnp.concatenate([high, small], axis=1), preferred_element_type=jnp.float32
                )
                code = (both[:, :128] * 256.0 + both[:, 128:] - 32768.0) * mine
                moved.append(code.reshape(PROJ, 8, 128))
            pair = jnp.concatenate(moved, axis=1)
            fsend[:, s] = pair.astype(jnp.int32).astype(jnp.int16)

        join_copy().start()

    def ship_fields():
        join_copy().wait()

        @pl.loop(0, CHIPS)
        def _(i):
            fjoin[i] = (
                fsend[core * CHIPS + i].astype(jnp.int32) + fpart[i].astype(jnp.int32)
            ).astype(jnp.int16)

        @pl.loop(1, CHIPS)
        def _(t):
            field_copy(t, away(2 * t) // 2).start()

        frecv[chip] = fjoin[chip]

    def take_fields():
        @pl.loop(1, CHIPS)
        def _(t):
            source = back(2 * t) // 2
            pltpu.make_async_remote_copy(
                src_ref=fjoin.at[source],
                dst_ref=frecv.at[source],
                send_sem=fsend_sem.at[t],
                recv_sem=frecv_sem.at[source],
                device_id=(2 * source + core, det),
                device_id_type=MESH,
            ).wait_recv()

        @pl.loop(0, SEGS)
        def _(s):
            total = frecv[0, s].astype(jnp.int32)
            for i in range(1, CHIPS):
                total = total + frecv[i, s].astype(jnp.int32)
            code = (total + 32768).astype(jnp.float32)
            f = 1.0 + code[:8] * FLAT_STEP
            d = code[8:] * DARK_STEP
            dark_s[s] = d
            logflat_s[s] = jnp.log(f - d)

    ship_frames(0)
    code_fields()
    ship_frames(1)
    ship_fields()
    ship_frames(2)
    ship_frames(3)
    take_fields()

    angle_id = (
        lax.broadcasted_iota(jnp.int32, (8, 128), 0) * 128
        + lax.broadcasted_iota(jnp.int32, (8, 128), 1)
    )

    def absorb(part, source, carry):
        acc0, acc1, places = carry
        accs = [acc0, acc1]
        for j in range(PAIRS):
            x = recv[part, source, j].astype(jnp.float32)
            for f in range(2):
                k = FRAMES * part + 2 * j + f
                here = slot_angle[SLOTS * source + k]
                pair = source + 1 - 2 * (source % 2)
                there = slot_angle[SLOTS * pair + SLOTS - 1 - k]
                angle = jnp.where(here < ANGLES, here, there)
                s = segment_of[angle]
                y = logflat_s[s] - jnp.log(x[8 * f : 8 * f + 8] - dark_s[s])
                y = y.astype(jnp.bfloat16).astype(jnp.float32)
                y_out[source * HALF + k] = y
                accs[f] = accs[f] + y
                places = jnp.where(angle_id == angle, source * HALF + k, places)
        return accs[0], accs[1], places

    zero = jnp.zeros((8, 128), jnp.float32)
    carry = (zero, zero, jnp.zeros((8, 128), jnp.int32))
    for part in range(PARTS):
        carry = absorb(part, proj, carry)

        def step(t, carry, part=part):
            source = back(t)
            pltpu.make_async_remote_copy(
                src_ref=send.at[part, 0],
                dst_ref=recv.at[part, source],
                send_sem=send_sem.at[part, t],
                recv_sem=recv_sem.at[part, source],
                device_id=(source, det),
                device_id_type=MESH,
            ).wait_recv()
            return absorb(part, source, carry)

        carry = lax.fori_loop(1, PROJ, step, carry)
    where_out[...] = carry[2]
    profile = (carry[0] + carry[1]) * (1.0 / ANGLES)

    def share(ref, which):
        copies = []
        for t in range(1, DET):
            copies.append(
                pltpu.make_async_remote_copy(
                    src_ref=ref.at[det],
                    dst_ref=ref.at[det],
                    send_sem=small_ssem.at[which, t],
                    recv_sem=small_rsem.at[which, det],
                    device_id=(proj, (det + t) % DET),
                    device_id_type=MESH,
                )
            )
            copies[-1].start()
        for t in range(1, DET):
            source = (det + t) % DET
            pltpu.make_async_remote_copy(
                src_ref=ref.at[source],
                dst_ref=ref.at[source],
                send_sem=small_ssem.at[which, t],
                recv_sem=small_rsem.at[which, source],
                device_id=(proj, source),
                device_id_type=MESH,
            ).wait_recv()
        return copies

    profs[det] = profile
    copies = share(profs, 0)
    sub = lax.broadcasted_iota(jnp.int32, (8, 128), 0)
    lane = lax.broadcasted_iota(jnp.int32, (8, 128), 1)
    before = profs[(det + DET - 1) % DET]
    after = profs[(det + 1) % DET]
    before = jnp.where(det > 0, before, jnp.zeros_like(before))
    after = jnp.where(det < DET - 1, after, jnp.zeros_like(after))
    low = jnp.where(sub < 2, pltpu.roll(before, 2, 0), pltpu.roll(profile, 2, 0))
    high = jnp.where(sub >= 6, pltpu.roll(after, 6, 0), pltpu.roll(profile, 6, 0))
    window = profile
    for o in range(1, RIM + 1):
        window = window + jnp.where(lane >= o, pltpu.roll(profile, o, 1), pltpu.roll(low, o, 1))
        window = window + jnp.where(
            lane < 128 - o, pltpu.roll(profile, 128 - o, 1), pltpu.roll(high, 128 - o, 1)
        )
    column = det * COLS_DEV + (sub // 2) * 128 + lane
    counted = jnp.minimum(column + RIM, COLS - 1) - jnp.maximum(column - RIM, 0) + 1
    delta = profile - window / counted.astype(jnp.float32)
    delta_out[...] = delta

    def magnitude(i, accs):
        return tuple(
            accs[u] + jnp.abs(y_out[i * 16 + u] - delta) + jnp.abs(y_out[i * 16 + 8 + u] - delta)
            for u in range(8)
        )

    accs = lax.fori_loop(0, ANGLES // 16, magnitude, (zero,) * 8)
    total = ((accs[0] + accs[1]) + (accs[2] + accs[3])) + ((accs[4] + accs[5]) + (accs[6] + accs[7]))
    sums[det] = total
    copies += share(sums, 1)
    total = (sums[0] + sums[1]) + (sums[2] + sums[3])
    rows = jnp.broadcast_to(jnp.sum(total, axis=1, keepdims=True), (8, 128))
    rows = rows + pltpu.roll(rows, 4, 0)
    rows = rows + pltpu.roll(rows, 2, 0)
    scale = rows * (1.0 / (ANGLES * COLS)) + EPSILON
    bins = jnp.where(
        sub % 2 == 0,
        bin_counts[row_order[2 * proj]],
        bin_counts[row_order[2 * proj + 1]],
    ).astype(jnp.float32)
    factor_out[...] = bins / scale

    for copy in copies:
        copy.wait_send()
    for copy in swaps:
        copy.wait_send()

    @pl.loop(1, CHIPS)
    def _(t):
        field_copy(t, away(2 * t) // 2).wait_send()

    for part in range(PARTS):

        @pl.loop(1, PROJ)
        def _(t, part=part):
            target = away(t)
            frame_copy(part, t, target, slot_of(target)).wait_send()


BLOCK = 128


def write_codes(places, y, delta, factor, out):
    start = pl.program_id(0) * BLOCK
    d, f = delta[...], factor[...]

    @pl.loop(0, BLOCK // 8)
    def _(i):
        for u in range(8):
            out[i * 8 + u] = (y[places[start + i * 8 + u]] - d) * f


def on_device(raw, slot_angle, segment_of, seg_owner, flat, dark, row_order, bin_counts):
    smem = pl.BlockSpec(memory_space=pltpu.SMEM)
    vmem = pl.BlockSpec(memory_space=pltpu.VMEM)
    hbm = pl.BlockSpec(memory_space=pl.ANY)
    tile = jax.ShapeDtypeStruct((8, 128), jnp.float32)
    dma = pltpu.SemaphoreType.DMA
    y, delta, factor, places = pl.pallas_call(
        exchange,
        name="exchange",
        out_shape=(
            jax.ShapeDtypeStruct((ANGLES, 8, 128), jnp.float32),
            tile,
            tile,
            jax.ShapeDtypeStruct((8, 128), jnp.int32),
        ),
        in_specs=[smem] * 5 + [hbm] * 3,
        out_specs=(vmem,) * 4,
        scratch_shapes=[
            pltpu.VMEM((HALF, ROWS, COLS_DEV), jnp.bfloat16),
            pltpu.VMEM((HALF, ROWS, COLS_DEV), jnp.bfloat16),
            pltpu.VMEM((PARTS, PROJ, PAIRS, 16, 128), jnp.bfloat16),
            pltpu.VMEM((PARTS, PROJ, PAIRS, 16, 128), jnp.bfloat16),
            pltpu.VMEM((SEGS, ROWS, COLS_DEV), jnp.float32),
            pltpu.VMEM((SEGS, ROWS, COLS_DEV), jnp.float32),
            pltpu.VMEM((256, 256), jnp.float32),
            pltpu.VMEM((256, 256), jnp.bfloat16),
            pltpu.VMEM((PROJ, SEGS, 16, 128), jnp.int16),
            pltpu.VMEM((CHIPS, SEGS, 16, 128), jnp.int16),
            pltpu.VMEM((CHIPS, SEGS, 16, 128), jnp.int16),
            pltpu.VMEM((CHIPS, SEGS, 16, 128), jnp.int16),
            pltpu.VMEM((SEGS, 8, 128), jnp.float32),
            pltpu.VMEM((SEGS, 8, 128), jnp.float32),
            pltpu.VMEM((DET, 8, 128), jnp.float32),
            pltpu.VMEM((DET, 8, 128), jnp.float32),
            dma((PARTS,)),
            dma((2,)),
            dma((PARTS,)),
            dma((PARTS,)),
            dma((PARTS, PROJ)),
            dma((PARTS, PROJ)),
            dma((2,)),
            dma((CHIPS,)),
            dma((CHIPS,)),
            dma((2, DET)),
            dma((2, DET)),
        ],
        compiler_params=pltpu.CompilerParams(
            collective_id=0, has_side_effects=True, vmem_limit_bytes=40 << 20
        ),
    )(slot_angle, segment_of, seg_owner, row_order, bin_counts, raw, flat, dark)
    whole = pl.BlockSpec((ANGLES, 8, 128), lambda i, places: (0, 0, 0))
    small = pl.BlockSpec((8, 128), lambda i, places: (0, 0))
    codes = pl.pallas_call(
        write_codes,
        name="write_codes",
        out_shape=jax.ShapeDtypeStruct((ANGLES, 8, 128), jnp.float32),
        grid_spec=pltpu.PrefetchScalarGridSpec(
            num_scalar_prefetch=1,
            grid=(ANGLES // BLOCK,),
            in_specs=[whole, small, small],
            out_specs=pl.BlockSpec((BLOCK, 8, 128), lambda i, places: (i, 0, 0)),
        ),
        compiler_params=pltpu.CompilerParams(vmem_limit_bytes=32 << 20),
    )(places.reshape(ANGLES), y, delta, factor)
    return codes.reshape(ANGLES, TILES, 2, 128).transpose(0, 2, 1, 3).reshape(ANGLES, 2, COLS_DEV)


def solution(mesh):
    return jax.shard_map(
        on_device,
        mesh=mesh,
        in_specs=(
            P("proj", None, "det"),
            P(),
            P(),
            P(),
            P("proj", None, "det"),
            P("proj", None, "det"),
            P(),
            P(),
        ),
        out_specs=P(None, "proj", "det"),
        check_vma=False,
    )
```

time: 297 us -> 68.7 us (0.23)
  waiting for transfers between devices: 162 us -> 0 us
  local copies, waits for them, and re-layouts: 72.7 us -> 7.98 us
  Pallas kernels: 0 us -> 60.4 us
  other arithmetic: 23.4 us -> 0 us
  between operations: 18.6 us -> 0.02 us
  starting transfers between devices: 10.1 us -> 0 us
  blocking collectives: 9.19 us -> 0 us
    psum x1 -> x0, waiting for transfers between devices: 105 us -> none  [broadcast(): return lax.psum(jnp.where(mine, x, jnp.zeros_like(x)), axis)]
    pallas_call x0 -> x2, Pallas kernels: none -> 60.4 us  [the longest x1 55.2 us: on_device(): pl.pallas_call(exchange, name='exchange', out_shape=(jax.ShapeDtypeStruct...]
    all_to_all x1 -> x0, waiting for transfers between devices: 53.2 us -> none  [on_device(): lax.all_to_all(ordered, 'proj', split_axis=1, concat_axis=0, tiled=True)]
    gather x6 -> x0, local copies, waits for them, and re-layouts: 23 us -> none  [the longest x1 8.07 us: place_by_angle(): return received[locate]]
    all_to_all x2 -> x0, local copies, waits for them, and re-layouts: 21.7 us -> none  [on_device(): lax.all_to_all(ordered, 'proj', split_axis=1, concat_axis=0, tiled=True)]
    psum x1 -> x0, blocking collectives: 9.19 us -> none  [on_device(): magnitude = lax.psum(jnp.sum(jnp.abs(corrected), axis=(0, 2)), 'det')]
    convert_element_type x2 -> x0, other arithmetic: 8.6 us -> none  [the longest x1 8.59 us: negative_log(): return (-jnp.log(ratio)).astype(jnp.bfloat16)]
    scatter x1 -> x0, local copies, waits for them, and re-layouts: 8.04 us -> none  [place_by_angle(): locate = jnp.zeros((total_angles,), jnp.int32).at[arrival].set(jnp.arange...]
  transfers between devices with their start and end apart: 4 -> 0, of which waited for: 3 -> 0; matrix products, arithmetic and copies ran while one was open for 3% -> 0% of each run, Pallas kernels for 0% -> 0%
where the time goes in v1:
time: 68.7 us; the launch traced here: 68.4 us
  Pallas kernels  60.4 us (88%)
  local copies, waits for them, and re-layouts  7.98 us (12%)
    pallas_call x1, Pallas kernels, on_device(): pl.pallas_call(exchange, name='exchange', out_shape=(jax.ShapeDtypeStruct...  55.2 us
    unnamed x16, local copies, waits for them, and re-layouts  7.98 us
    pallas_call x1, Pallas kernels, on_device(): pl.pallas_call(write_codes, name='write_codes', out_shape=jax.ShapeDtypeS...  5.14 us

profile of v1, /device:TPU:0, one launch (start us, length us, event | category | flops | bytes accessed | tf_op | source)
XLA Modules:
  0.0 68.4 jit_solution(13771152814049296342)
XLA Ops:
  0.0 0.0 copy-start
  0.0 2.2 %copy-done = bf16[64,64,512]{2,1,0:T(8,128)(2,1)S(1)} copy-done((bf16[64,64,512]{2,1,0:T(8,128)(2,1)S(1)}, bf16[64,64,512]{2,1,0:T(8,128)(2,1)}, u32[]{:S(2)}) %copy-start) | copy-done | bytes 4194328
  2.2 0.0 copy-start.1
  2.2 1.2 %copy-done.1 = f32[8,64,512]{2,1,0:T(8,128)S(1)} copy-done((f32[8,64,512]{2,1,0:T(8,128)S(1)}, f32[8,64,512]{2,1,0:T(8,128)}, u32[]{:S(2)}) %copy-start.1) | copy-done | bytes 1048600
  3.4 0.0 copy-start.2
  3.4 1.2 %copy-done.2 = f32[8,64,512]{2,1,0:T(8,128)S(1)} copy-done((f32[8,64,512]{2,1,0:T(8,128)S(1)}, f32[8,64,512]{2,1,0:T(8,128)}, u32[]{:S(2)}) %copy-start.2) | copy-done | bytes 1048600
  4.6 0.0 copy-start.3
  4.6 0.7 %copy-done.3 = s32[2048]{0:T(1024)S(1)} copy-done((s32[2048]{0:T(1024)S(1)}, s32[2048]{0:T(1024)}, u32[]{:S(2)}) %copy-start.3) | copy-done | bytes 8216
  5.3 0.0 copy-start.4
  5.3 0.7 %copy-done.4 = s32[1024]{0:T(1024)S(1)} copy-done((s32[1024]{0:T(1024)S(1)}, s32[1024]{0:T(1024)}, u32[]{:S(2)}) %copy-start.4) | copy-done | bytes 4120
  6.0 0.0 copy-start.5
  6.0 0.7 copy-done.5
  6.7 0.0 copy-start.6
  6.7 0.7 copy-done.6
  7.3 0.0 copy-start.7
  7.3 0.7 copy-done.7
  8.0 55.2 %exchange.1 = (f32[1024,8,128]{2,1,0:T(8,128)S(1)}, f32[8,128]{1,0:T(8,128)S(1)}, f32[8,128]{1,0:T(8,128)S(1)}, s32[8,128]{1,0:T(8,128)S(1)}) custom-call(s32[2048]{0:T(1024)S(1)} %copy-done.3, s32[1024]{0:T(1024)S(1)} %copy-done.4, s32[8]{0:T(128)S(1)} %copy-done.5, s32[64]{0:T(128)S(1)} %copy-done.6, s32[64]{0:T(128)S(1)} %copy-done.7, ...), custom_call_target="tpu_custom_call" | custom-call | tf_op jit(solution)/shard_map/exchange/pallas_call | solution.py:433
  63.2 5.1 %write_codes.1 = f32[1024,8,128]{2,1,0:T(8,128)} custom-call(s32[1024]{0:T(1024)S(1)} %bitcast.6, f32[1024,8,128]{2,1,0:T(8,128)S(1)} %get-tuple-element.10.y, f32[8,128]{1,0:T(8,128)S(1)} %get-tuple-element.11.delta, f32[8,128]{1,0:T(8,128)S(1)} %get-tuple-element.12.factor), custom_call_target="tpu_custom_call" | custom-call | tf_op jit(solution)/shard_map/write_codes/pallas_call | solution.py:479
Async XLA Ops:
  0.0 2.2 %copy-start = (bf16[64,64,512]{2,1,0:T(8,128)(2,1)S(1)}, bf16[64,64,512]{2,1,0:T(8,128)(2,1)}, u32[]{:S(2)}) copy-start(bf16[64,64,512]{2,1,0:T(8,128)(2,1)} %raw.1) | copy-start | bytes 12582916
  2.2 1.2 %copy-start.1 = (f32[8,64,512]{2,1,0:T(8,128)S(1)}, f32[8,64,512]{2,1,0:T(8,128)}, u32[]{:S(2)}) copy-start(f32[8,64,512]{2,1,0:T(8,128)} %flat.1) | copy-start | bytes 3145732
  3.4 1.2 %copy-start.2 = (f32[8,64,512]{2,1,0:T(8,128)S(1)}, f32[8,64,512]{2,1,0:T(8,128)}, u32[]{:S(2)}) copy-start(f32[8,64,512]{2,1,0:T(8,128)} %dark.1) | copy-start | bytes 3145732
  4.6 0.7 %copy-start.3 = (s32[2048]{0:T(1024)S(1)}, s32[2048]{0:T(1024)}, u32[]{:S(2)}) copy-start(s32[2048]{0:T(1024)} %slot_angle.1) | copy-start | bytes 24580
  5.3 0.7 %copy-start.4 = (s32[1024]{0:T(1024)S(1)}, s32[1024]{0:T(1024)}, u32[]{:S(2)}) copy-start(s32[1024]{0:T(1024)} %segment_of.1) | copy-start | bytes 12292
  6.0 0.7 copy-start.5
  6.7 0.7 copy-start.6
  7.3 0.7 copy-start.7

commit v2 on v1

v2 whole, which is shorter than its diff:
```python
import jax
import jax.numpy as jnp
from jax import lax
from jax.experimental import pallas as pl
from jax.experimental.pallas import tpu as pltpu
from jax.sharding import PartitionSpec as P

MESH = pl.DeviceIdType.MESH

SLOTS = 64
ANGLES = 1024
ROWS = 64
COLS_DEV = 512
COLS = 2048
SEGS = 8
RIM = 8
PROJ = 32
CHIPS = 16
DET = 4
TILES = COLS_DEV // 128
PARTS = 8
FRAMES = SLOTS // PARTS
PAIRS = FRAMES // 2
EARLY = 4
EPSILON = 1e-6
DARK_STEP = 0.2 / 65535.0
FLAT_STEP = 1.0 / 65535.0
STEPS = (
    (2, 2), (1, 2), (2, 1), (3, 2), (2, 3), (1, 1), (3, 3), (1, 3),
    (3, 1), (0, 2), (2, 0), (0, 1), (1, 0), (0, 3), (3, 0),
)


def stack_tiles(frame):
    return jnp.concatenate([frame[:, 128 * t : 128 * (t + 1)] for t in range(TILES)], axis=0)


def coded(field, low, step):
    q = jnp.floor((field - low) * (1.0 / step) + 0.5)
    q = jnp.clip(q, 0.0, 65535.0)
    high = jnp.floor(q * (1.0 / 256.0))
    return high.astype(jnp.bfloat16), (q - 256.0 * high).astype(jnp.bfloat16)


def exchange(
    slot_angle_h,
    segment_of_h,
    seg_owner_h,
    row_order_h,
    bin_counts_h,
    raw,
    flat,
    dark,
    corrected_out,
    factor_out,
    slot_angle,
    segment_of,
    seg_owner,
    row_order,
    bin_counts,
    segs,
    places,
    places_v,
    frames,
    own,
    away,
    mate_in,
    recv,
    y_v,
    flat_v,
    dark_v,
    pick_f,
    pick,
    fsend,
    fpart,
    frecv,
    dark_s,
    logflat_s,
    profs,
    sums,
    int_sem,
    load_sem,
    field_sem,
    place_sem,
    swap_ssem,
    swap_rsem,
    send_sem,
    recv_sem,
    fswap_sem,
    fsend_sem,
    frecv_sem,
    small_ssem,
    small_rsem,
):
    proj = lax.axis_index("proj")
    det = lax.axis_index("det")
    core = proj % 2
    chip = proj // 2
    col = chip % 4
    lay = chip // 4
    mate = proj + 1 - 2 * core

    def chip_at(step):
        return (lay + step[0]) % 4 * 4 + (col + step[1]) % 4

    def chip_back(t):
        return (lay + 4 - t // 4) % 4 * 4 + (col + 4 - t % 4) % 4

    ints = []
    for i, (source, target) in enumerate(
        (
            (row_order_h, row_order),
            (slot_angle_h, slot_angle),
            (seg_owner_h, seg_owner),
            (segment_of_h, segment_of),
            (bin_counts_h, bin_counts),
        )
    ):
        ints.append(pltpu.make_async_copy(source, target, int_sem.at[i]))
        ints[-1].start()
    order = [q for i in range(PARTS // 2) for q in (PARTS - 1 - i, i)]
    loads = {}
    for q in order:
        block = pl.ds(FRAMES * q, FRAMES)
        loads[q] = pltpu.make_async_copy(raw.at[block], frames.at[block], load_sem.at[q])
        loads[q].start()
    flat_copy = pltpu.make_async_copy(flat, flat_v, field_sem.at[0])
    dark_copy = pltpu.make_async_copy(dark, dark_v, field_sem.at[1])
    flat_copy.start()
    dark_copy.start()

    barrier = pltpu.get_barrier_semaphore()
    for step in STEPS:
        pl.semaphore_signal(
            barrier, inc=1, device_id=(2 * chip_at(step) + core, det), device_id_type=MESH
        )
    for t in range(1, DET):
        pl.semaphore_signal(
            barrier, inc=1, device_id=(proj, (det + t) % DET), device_id_type=MESH
        )
    pl.semaphore_signal(barrier, inc=1, device_id=(mate, det), device_id_type=MESH)

    for copy in ints:
        copy.wait()

    sub = lax.broadcasted_iota(jnp.int32, (8, 256), 0)
    lane = lax.broadcasted_iota(jnp.int32, (8, 256), 1)

    @pl.loop(0, PROJ)
    def _(i):
        p = 2 * (i % CHIPS) + (core + i // CHIPS) % 2
        row = jnp.where(sub % 2 == 0, row_order[2 * p], row_order[2 * p + 1])
        hit = lane == row + (sub // 2) * ROWS
        pick_f[pl.ds(pl.multiple_of(8 * i, 8), 8), :] = jnp.where(hit, 1.0, 0.0)

    pick[...] = pick_f[...].astype(jnp.bfloat16)

    def permute(q):
        loads[q].wait()

        @pl.loop(0, PAIRS)
        def _(j):
            first = stack_tiles(frames[FRAMES * q + 2 * j])
            second = stack_tiles(frames[FRAMES * q + 2 * j + 1])
            moved = jnp.dot(
                pick[...], jnp.concatenate([first, second], axis=1), preferred_element_type=jnp.float32
            ).reshape(PROJ, 8, 256)
            here, there = moved[:CHIPS], moved[CHIPS:]
            own[q, :, j] = jnp.concatenate([here[:, :, :128], here[:, :, 128:]], axis=1).astype(
                jnp.bfloat16
            )
            away[PARTS - 1 - q, :, PAIRS - 1 - j] = jnp.concatenate(
                [there[:, :, 128:], there[:, :, :128]], axis=1
            ).astype(jnp.bfloat16)

    def swap(part):
        return pltpu.make_async_remote_copy(
            src_ref=away.at[part],
            dst_ref=mate_in.at[part],
            send_sem=swap_ssem.at[part],
            recv_sem=swap_rsem.at[part],
            device_id=(mate, det),
            device_id_type=MESH,
        )

    sub16 = lax.broadcasted_iota(jnp.int32, (16, 128), 0)

    def merge(part):
        swap(part).wait_recv()

        @pl.loop(0, PAIRS)
        def _(j):
            k = SLOTS * proj + FRAMES * part + 2 * j
            keep = jnp.where(
                sub16 < 8,
                jnp.where(slot_angle[k] < ANGLES, 1.0, 0.0),
                jnp.where(slot_angle[k + 1] < ANGLES, 1.0, 0.0),
            )
            mine = keep.astype(jnp.bfloat16)
            other = (1.0 - keep).astype(jnp.bfloat16)
            own[part, :, j] = own[part, :, j] * mine + mate_in[part, :, j] * other

    def frame_copy(part, t, target):
        return pltpu.make_async_remote_copy(
            src_ref=own.at[part, target],
            dst_ref=recv.at[part, chip],
            send_sem=send_sem.at[part, t],
            recv_sem=recv_sem.at[part, chip],
            device_id=(2 * target + core, det),
            device_id_type=MESH,
        )

    def ship(part):
        merge(part)
        for t, step in enumerate(STEPS):
            frame_copy(part, t, chip_at(step)).start()

    def join_copy():
        return pltpu.make_async_remote_copy(
            src_ref=fsend.at[pl.ds(CHIPS, CHIPS)],
            dst_ref=fpart,
            send_sem=fswap_sem.at[0],
            recv_sem=fswap_sem.at[1],
            device_id=(mate, det),
            device_id_type=MESH,
        )

    def field_copy(t, target):
        return pltpu.make_async_remote_copy(
            src_ref=fsend.at[target],
            dst_ref=frecv.at[chip],
            send_sem=fsend_sem.at[t],
            recv_sem=frecv_sem.at[chip],
            device_id=(2 * target + core, det),
            device_id_type=MESH,
        )

    def code_fields():
        flat_copy.wait()
        dark_copy.wait()

        @pl.loop(0, SEGS)
        def _(s):
            mine = jnp.where(seg_owner[s] == proj, 1.0, 0.0)
            moved = []
            for ref, low, step in ((flat_v, 1.0, FLAT_STEP), (dark_v, 0.0, DARK_STEP)):
                high, small = coded(stack_tiles(ref[s]), low, step)
                both = jnp.dot(
                    pick[...], jnp.concatenate([high, small], axis=1), preferred_element_type=jnp.float32
                )
                code = (both[:, :128] * 256.0 + both[:, 128:] - 32768.0) * mine
                moved.append(code.reshape(PROJ, 8, 128))
            pair = jnp.concatenate(moved, axis=1)
            fsend[:, s] = pair.astype(jnp.int32).astype(jnp.int16)

        join_copy().start()

    def ship_fields():
        join_copy().wait()

        @pl.loop(0, CHIPS)
        def _(i):
            fsend[i] = (fsend[i].astype(jnp.int32) + fpart[i].astype(jnp.int32)).astype(jnp.int16)

        for t, step in enumerate(STEPS):
            field_copy(t, chip_at(step)).start()
        frecv[chip] = fsend[chip]

    def take_fields():
        @pl.loop(1, CHIPS)
        def _(t):
            source = chip_back(t)
            pltpu.make_async_remote_copy(
                src_ref=fsend.at[source],
                dst_ref=frecv.at[source],
                send_sem=fsend_sem.at[t - 1],
                recv_sem=frecv_sem.at[source],
                device_id=(2 * source + core, det),
                device_id_type=MESH,
            ).wait()

        @pl.loop(0, SEGS)
        def _(s):
            total = frecv[0, s].astype(jnp.int32)
            for i in range(1, CHIPS):
                total = total + frecv[i, s].astype(jnp.int32)
            code = (total + 32768).astype(jnp.float32)
            f = 1.0 + code[:8] * FLAT_STEP
            d = code[8:] * DARK_STEP
            dark_s[s] = d
            logflat_s[s] = jnp.log(f - d)

    for q in order[:EARLY]:
        permute(q)
    pl.semaphore_wait(barrier, len(STEPS) + DET)
    for q in order[:EARLY]:
        swap(PARTS - 1 - q).start()

    def more(q):
        permute(q)
        swap(PARTS - 1 - q).start()

    ship(0)
    more(order[4])
    ship(1)
    more(order[5])
    code_fields()
    ship(2)
    more(order[6])
    ship_fields()
    more(order[7])
    for part in range(3, PARTS):
        ship(part)

    sub = lax.broadcasted_iota(jnp.int32, (8, 128), 0)
    lane = lax.broadcasted_iota(jnp.int32, (8, 128), 1)
    angle_id = sub * 128 + lane

    def locate(i, found):
        source = 2 * (i // (SLOTS // 4)) + core
        pair = source + 1 - 2 * core
        found = list(found)
        for u in range(4):
            k = i % (SLOTS // 4) * 4 + u
            here = slot_angle[SLOTS * source + k]
            there = slot_angle[SLOTS * pair + SLOTS - 1 - k]
            angle = jnp.where(here < ANGLES, here, there)
            segs[i * 4 + u] = segment_of[angle]
            found[u] = jnp.where(angle_id == angle, i * 4 + u, found[u])
        return tuple(found)

    found = lax.fori_loop(0, ANGLES // 4, locate, (jnp.zeros((8, 128), jnp.int32),) * 4)
    places_v[...] = jnp.maximum(jnp.maximum(found[0], found[1]), jnp.maximum(found[2], found[3]))
    place_copy = pltpu.make_async_copy(places_v, places, place_sem.at[0])
    place_copy.start()

    take_fields()

    def absorb(ref, part, source, accs):
        accs = list(accs)
        for j in range(PAIRS):
            x = ref[part, source, j].astype(jnp.float32)
            for f in range(2):
                slot = source * SLOTS + FRAMES * part + 2 * j + f
                s = segs[slot]
                y = logflat_s[s] - jnp.log(x[8 * f : 8 * f + 8] - dark_s[s])
                y = y.astype(jnp.bfloat16).astype(jnp.float32)
                y_v[slot] = y
                accs[f] = accs[f] + y
        return tuple(accs)

    zero = jnp.zeros((8, 128), jnp.float32)
    accs = (zero, zero)
    for part in range(PARTS):
        accs = absorb(own, part, chip, accs)

        def step(t, accs, part=part):
            source = chip_back(t)
            pltpu.make_async_remote_copy(
                src_ref=own.at[part, source],
                dst_ref=recv.at[part, source],
                send_sem=send_sem.at[part, t - 1],
                recv_sem=recv_sem.at[part, source],
                device_id=(2 * source + core, det),
                device_id_type=MESH,
            ).wait()
            return absorb(recv, part, source, accs)

        accs = lax.fori_loop(1, CHIPS, step, accs)
        swap(part).wait_send()
    place_copy.wait()
    profile = (accs[0] + accs[1]) * (1.0 / ANGLES)

    def share(ref, which, t):
        return pltpu.make_async_remote_copy(
            src_ref=ref.at[det],
            dst_ref=ref.at[det],
            send_sem=small_ssem.at[which, t],
            recv_sem=small_rsem.at[which, det],
            device_id=(proj, (det + t) % DET),
            device_id_type=MESH,
        )

    def shared(ref, which, t):
        source = (det + t) % DET
        return pltpu.make_async_remote_copy(
            src_ref=ref.at[source],
            dst_ref=ref.at[source],
            send_sem=small_ssem.at[which, t],
            recv_sem=small_rsem.at[which, source],
            device_id=(proj, source),
            device_id_type=MESH,
        )

    profs[det] = profile
    for t in (1, 3, 2):
        share(profs, 0, t).start()
    shared(profs, 0, 1).wait_recv()
    shared(profs, 0, 3).wait_recv()
    shared(profs, 0, 2).wait_recv()
    before = profs[(det + DET - 1) % DET]
    after = profs[(det + 1) % DET]
    before = jnp.where(det > 0, before, jnp.zeros_like(before))
    after = jnp.where(det < DET - 1, after, jnp.zeros_like(after))
    low = jnp.where(sub < 2, pltpu.roll(before, 2, 0), pltpu.roll(profile, 2, 0))
    high = jnp.where(sub >= 6, pltpu.roll(after, 6, 0), pltpu.roll(profile, 6, 0))
    window = profile
    for o in range(1, RIM + 1):
        window = window + jnp.where(lane >= o, pltpu.roll(profile, o, 1), pltpu.roll(low, o, 1))
        window = window + jnp.where(
            lane < 128 - o, pltpu.roll(profile, 128 - o, 1), pltpu.roll(high, 128 - o, 1)
        )
    column = det * COLS_DEV + (sub // 2) * 128 + lane
    counted = jnp.minimum(column + RIM, COLS - 1) - jnp.maximum(column - RIM, 0) + 1
    delta = profile - window / counted.astype(jnp.float32)

    def magnitude(i, accs):
        return tuple(
            accs[u] + jnp.abs(y_v[i * 16 + u] - delta) + jnp.abs(y_v[i * 16 + 8 + u] - delta)
            for u in range(8)
        )

    accs = lax.fori_loop(0, ANGLES // 16, magnitude, (zero,) * 8)
    total = ((accs[0] + accs[1]) + (accs[2] + accs[3])) + ((accs[4] + accs[5]) + (accs[6] + accs[7]))
    sums[det] = total
    for t in (2, 1, 3):
        share(sums, 1, t).start()

    @pl.loop(0, ANGLES // 16)
    def _(i):
        for u in range(16):
            a = 16 * (i % 8) + u
            corrected_out[i * 16 + u] = y_v[places[i // 8, a]] - delta

    for t in range(1, DET):
        shared(sums, 1, t).wait_recv()
    total = (sums[0] + sums[1]) + (sums[2] + sums[3])
    rows = jnp.broadcast_to(jnp.sum(total, axis=1, keepdims=True), (8, 128))
    rows = rows + pltpu.roll(rows, 4, 0)
    rows = rows + pltpu.roll(rows, 2, 0)
    scale = rows * (1.0 / (ANGLES * COLS)) + EPSILON
    bins = jnp.where(
        sub % 2 == 0,
        bin_counts[row_order[2 * proj]],
        bin_counts[row_order[2 * proj + 1]],
    ).astype(jnp.float32)
    factor_out[...] = bins / scale

    for which, ref in enumerate((profs, sums)):
        for t in range(1, DET):
            share(ref, which, t).wait_send()


BLOCK = 128
DEPTH = 4


def write_codes(corrected, factor, out, block, sem):
    f = factor[...]

    def copy(i):
        return pltpu.make_async_copy(
            block.at[i % DEPTH], out.at[pl.ds(i * BLOCK, BLOCK)], sem.at[i % DEPTH]
        )

    @pl.loop(0, ANGLES // BLOCK)
    def _(i):
        @pl.when(i >= DEPTH)
        def _():
            copy(i - DEPTH).wait()

        @pl.loop(0, BLOCK // 16)
        def _(k):
            for u in range(16):
                block[i % DEPTH, k * 16 + u] = corrected[i * BLOCK + k * 16 + u] * f

        copy(i).start()

    @pl.loop(ANGLES // BLOCK - DEPTH, ANGLES // BLOCK)
    def _(i):
        copy(i).wait()


def on_device(raw, slot_angle, segment_of, seg_owner, flat, dark, row_order, bin_counts):
    vmem = pl.BlockSpec(memory_space=pltpu.VMEM)
    hbm = pl.BlockSpec(memory_space=pltpu.HBM)
    dma = pltpu.SemaphoreType.DMA
    corrected, factor = pl.pallas_call(
        exchange,
        name="exchange",
        out_shape=(
            jax.ShapeDtypeStruct((ANGLES, 8, 128), jnp.float32),
            jax.ShapeDtypeStruct((8, 128), jnp.float32),
        ),
        in_specs=[hbm] * 8,
        out_specs=(vmem,) * 2,
        scratch_shapes=[
            pltpu.SMEM((PROJ * SLOTS,), jnp.int32),
            pltpu.SMEM((ANGLES,), jnp.int32),
            pltpu.SMEM((SEGS,), jnp.int32),
            pltpu.SMEM((ROWS,), jnp.int32),
            pltpu.SMEM((ROWS,), jnp.int32),
            pltpu.SMEM((ANGLES,), jnp.int32),
            pltpu.SMEM((8, 128), jnp.int32),
            pltpu.VMEM((8, 128), jnp.int32),
            pltpu.VMEM((SLOTS, ROWS, COLS_DEV), jnp.bfloat16),
            pltpu.VMEM((PARTS, CHIPS, PAIRS, 16, 128), jnp.bfloat16),
            pltpu.VMEM((PARTS, CHIPS, PAIRS, 16, 128), jnp.bfloat16),
            pltpu.VMEM((PARTS, CHIPS, PAIRS, 16, 128), jnp.bfloat16),
            pltpu.VMEM((PARTS, CHIPS, PAIRS, 16, 128), jnp.bfloat16),
            pltpu.VMEM((ANGLES, 8, 128), jnp.float32),
            pltpu.VMEM((SEGS, ROWS, COLS_DEV), jnp.float32),
            pltpu.VMEM((SEGS, ROWS, COLS_DEV), jnp.float32),
            pltpu.VMEM((256, 256), jnp.float32),
            pltpu.VMEM((256, 256), jnp.bfloat16),
            pltpu.VMEM((PROJ, SEGS, 16, 128), jnp.int16),
            pltpu.VMEM((CHIPS, SEGS, 16, 128), jnp.int16),
            pltpu.VMEM((CHIPS, SEGS, 16, 128), jnp.int16),
            pltpu.VMEM((SEGS, 8, 128), jnp.float32),
            pltpu.VMEM((SEGS, 8, 128), jnp.float32),
            pltpu.VMEM((DET, 8, 128), jnp.float32),
            pltpu.VMEM((DET, 8, 128), jnp.float32),
            dma((5,)),
            dma((PARTS,)),
            dma((2,)),
            dma((1,)),
            dma((PARTS,)),
            dma((PARTS,)),
            dma((PARTS, CHIPS)),
            dma((PARTS, CHIPS)),
            dma((2,)),
            dma((CHIPS,)),
            dma((CHIPS,)),
            dma((2, DET)),
            dma((2, DET)),
        ],
        compiler_params=pltpu.CompilerParams(
            collective_id=0, has_side_effects=True, vmem_limit_bytes=40 << 20
        ),
    )(
        *(
            pltpu.with_memory_space_constraint(a, pltpu.HBM)
            for a in (slot_angle, segment_of, seg_owner, row_order, bin_counts, raw, flat, dark)
        )
    )
    codes = pl.pallas_call(
        write_codes,
        name="write_codes",
        out_shape=jax.ShapeDtypeStruct((ANGLES, 8, 128), jnp.float32),
        in_specs=[vmem, vmem],
        out_specs=hbm,
        scratch_shapes=[pltpu.VMEM((DEPTH, BLOCK, 8, 128), jnp.float32), dma((DEPTH,))],
        compiler_params=pltpu.CompilerParams(vmem_limit_bytes=16 << 20),
    )(corrected, factor)
    return codes.reshape(ANGLES, TILES, 2, 128).transpose(0, 2, 1, 3).reshape(ANGLES, 2, COLS_DEV)


def solution(mesh):
    return jax.shard_map(
        on_device,
        mesh=mesh,
        in_specs=(
            P("proj", None, "det"),
            P(),
            P(),
            P(),
            P("proj", None, "det"),
            P("proj", None, "det"),
            P(),
            P(),
        ),
        out_specs=P(None, "proj", "det"),
        check_vma=False,
    )
```

time: 68.7 us -> 55.5 us (0.81)
  local copies, waits for them, and re-layouts: 7.98 us -> 0 us
  Pallas kernels: 60.4 us -> 55.3 us
    unnamed x16 -> x0, local copies, waits for them, and re-layouts: 7.98 us -> none
    pallas_call x1, Pallas kernels: 5.14 us -> 2.31 us  [on_device(): pl.pallas_call(write_codes, name='write_codes', out_shape=jax.ShapeDtypeS...]
    pallas_call x1, Pallas kernels: 55.2 us -> 53 us  [on_device(): pl.pallas_call(exchange, name='exchange', out_shape=(jax.ShapeDtypeStruct...]
where the time goes in v2:
time: 55.5 us; the launch traced here: 55.3 us
  Pallas kernels  55.3 us (100%)
    pallas_call x1, Pallas kernels, on_device(): pl.pallas_call(exchange, name='exchange', out_shape=(jax.ShapeDtypeStruct...  53 us
    pallas_call x1, Pallas kernels, on_device(): pl.pallas_call(write_codes, name='write_codes', out_shape=jax.ShapeDtypeS...  2.31 us

profile of v2, /device:TPU:0, one launch (start us, length us, event | category | flops | bytes accessed | tf_op | source)
XLA Modules:
  0.0 55.3 jit_solution(3079096655621215668)
XLA Ops:
  0.0 53.0 %exchange.1 = (f32[1024,8,128]{2,1,0:T(8,128)S(1)}, f32[8,128]{1,0:T(8,128)S(1)}) custom-call(s32[2048]{0:T(1024)} %slot_angle_h.1, s32[1024]{0:T(1024)} %segment_of_h.1, s32[8]{0:T(128)} %seg_owner_h.1, s32[64]{0:T(128)} %row_order_h.1, s32[64]{0:T(128)} %bin_counts_h.1, bf16[64,64,512]{2,1,0:T(8,128)(2,1)} %raw.1, f32[8,64,512]{2,1,0:T(8,128)} %flat.1, ...), custom_call_target="tpu_custom_call" | custom-call | tf_op jit(solution)/shard_map/exchange/pallas_call | solution.py:488
  53.0 2.3 %write_codes.1 = f32[1024,8,128]{2,1,0:T(8,128)} custom-call(f32[1024,8,128]{2,1,0:T(8,128)S(1)} %get-tuple-element.7.corrected, f32[8,128]{1,0:T(8,128)S(1)} %get-tuple-element.8.factor), custom_call_target="tpu_custom_call" | custom-call | tf_op jit(solution)/shard_map/write_codes/pallas_call | solution.py:546

commit v3 on v2

v3 whole, which is shorter than its diff:
```python
import jax
import jax.numpy as jnp
from jax import lax
from jax.experimental import pallas as pl
from jax.experimental.pallas import tpu as pltpu
from jax.sharding import PartitionSpec as P

MESH = pl.DeviceIdType.MESH

SLOTS = 64
ANGLES = 1024
ROWS = 64
COLS_DEV = 512
COLS = 2048
SEGS = 8
RIM = 8
PROJ = 32
CHIPS = 16
DET = 4
TILES = COLS_DEV // 128
PARTS = 8
FRAMES = SLOTS // PARTS
PAIRS = FRAMES // 2
HEAD = 1
BATCH = 4
ARRANGED = 20
HALVES = 2
RING = 4
HSEGS = SEGS // HALVES
EPSILON = 1e-6
DARK_STEP = 0.2 / 65535.0
FLAT_STEP = 1.0 / 65535.0
STEPS = (
    (2, 2), (1, 2), (2, 1), (3, 2), (2, 3), (1, 1), (3, 3), (1, 3),
    (3, 1), (0, 2), (2, 0), (0, 1), (1, 0), (0, 3), (3, 0),
)


def stack_tiles(frame):
    return jnp.concatenate([frame[:, 128 * t : 128 * (t + 1)] for t in range(TILES)], axis=0)


def coded(field, low, step):
    q = jnp.floor((field - low) * (1.0 / step) + 0.5)
    q = jnp.clip(q, 0.0, 65535.0)
    high = jnp.floor(q * (1.0 / 256.0))
    return high.astype(jnp.bfloat16), (q - 256.0 * high).astype(jnp.bfloat16)


def exchange(
    slot_angle_h,
    segment_of_h,
    seg_owner_h,
    row_order_h,
    bin_counts_h,
    raw,
    flat,
    dark,
    ordered_out,
    delta_out,
    factor_out,
    slot_angle,
    seg_owner,
    row_order,
    bin_counts,
    angle_v,
    segment_v,
    segs,
    segs_v,
    places,
    places_v,
    frames,
    own,
    away,
    mate_in,
    recv,
    y_v,
    flat_v,
    dark_v,
    pick_f,
    pick,
    fsend,
    fmate,
    fpart,
    fring,
    fnext,
    flast,
    edges,
    dark_s,
    logflat_s,
    profs,
    sums,
    int_sem,
    load_sem,
    field_sem,
    place_sem,
    swap_ssem,
    swap_rsem,
    send_sem,
    recv_sem,
    fswap_sem,
    fring_sem,
    flast_sem,
    small_sem,
):
    proj = lax.axis_index("proj")
    det = lax.axis_index("det")
    core = proj % 2
    chip = proj // 2
    col = chip % 4
    lay = chip // 4
    mate = proj + 1 - 2 * core

    def chip_at(step):
        return (lay + step[0]) % 4 * 4 + (col + step[1]) % 4

    barrier = pltpu.get_barrier_semaphore()
    for step in STEPS:
        pl.semaphore_signal(
            barrier, inc=1, device_id=(2 * chip_at(step) + core, det), device_id_type=MESH
        )
    for t in range(1, DET):
        pl.semaphore_signal(
            barrier, inc=1, device_id=(proj, (det + t) % DET), device_id_type=MESH
        )
    pl.semaphore_signal(barrier, inc=1, device_id=(mate, det), device_id_type=MESH)

    ints = []
    for i, (source, target) in enumerate(
        (
            (row_order_h, row_order),
            (slot_angle_h, slot_angle),
            (seg_owner_h, seg_owner),
            (bin_counts_h, bin_counts),
            (slot_angle_h, angle_v),
            (segment_of_h, segment_v),
        )
    ):
        ints.append(pltpu.make_async_copy(source, target, int_sem.at[i]))
        ints[-1].start()
    order = [q for i in range(PARTS // 2) for q in (PARTS - 1 - i, i)]
    loads = {}
    for q in order:
        block = pl.ds(FRAMES * q, FRAMES)
        loads[q] = pltpu.make_async_copy(raw.at[block], frames.at[block], load_sem.at[q])
        loads[q].start()
    flat_copy = pltpu.make_async_copy(flat, flat_v, field_sem.at[0])
    dark_copy = pltpu.make_async_copy(dark, dark_v, field_sem.at[1])
    flat_copy.start()
    dark_copy.start()

    for copy in ints:
        copy.wait()

    sub = lax.broadcasted_iota(jnp.int32, (8, 256), 0)
    lane = lax.broadcasted_iota(jnp.int32, (8, 256), 1)

    @pl.loop(0, PROJ)
    def _(i):
        p = 2 * (i % CHIPS) + (core + i // CHIPS) % 2
        row = jnp.where(sub % 2 == 0, row_order[2 * p], row_order[2 * p + 1])
        hit = lane == row + (sub // 2) * ROWS
        pick_f[pl.ds(pl.multiple_of(8 * i, 8), 8), :] = jnp.where(hit, 1.0, 0.0)

    pick[...] = pick_f[...].astype(jnp.bfloat16)

    def permute(q):
        loads[q].wait()

        @pl.loop(0, PAIRS // 2)
        def _(i):
            block = [stack_tiles(frames[FRAMES * q + 4 * i + f]) for f in range(4)]
            moved = jnp.dot(
                pick[...], jnp.concatenate(block, axis=1), preferred_element_type=jnp.float32
            ).reshape(PROJ, 8, 512)
            part = [moved[:, :, 128 * f : 128 * (f + 1)] for f in range(4)]
            for j in range(2):
                first, second = part[2 * j], part[2 * j + 1]
                own[q, :, 2 * i + j] = jnp.concatenate(
                    [first[:CHIPS], second[:CHIPS]], axis=1
                ).astype(jnp.bfloat16)
                away[PARTS - 1 - q, :, PAIRS - 1 - 2 * i - j] = jnp.concatenate(
                    [second[CHIPS:], first[CHIPS:]], axis=1
                ).astype(jnp.bfloat16)

    def swap(part, first=0, count=PAIRS, which=None):
        which = part if which is None else which
        pairs = pl.ds(first, count)
        return pltpu.make_async_remote_copy(
            src_ref=away.at[part, :, pairs],
            dst_ref=mate_in.at[part, :, pairs],
            send_sem=swap_ssem.at[which],
            recv_sem=swap_rsem.at[which],
            device_id=(mate, det),
            device_id_type=MESH,
        )

    pieces = ((0, HEAD, PARTS), (HEAD, PAIRS - HEAD, 0))

    sub16 = lax.broadcasted_iota(jnp.int32, (16, 128), 0)

    def merge(part, first=0, count=PAIRS):
        @pl.loop(first, first + count)
        def _(j):
            k = SLOTS * core + FRAMES * part + 2 * j
            keep = jnp.where(
                sub16 < 8,
                jnp.where(slot_angle[chip, k] < ANGLES, 1.0, 0.0),
                jnp.where(slot_angle[chip, k + 1] < ANGLES, 1.0, 0.0),
            )
            mine = keep.astype(jnp.bfloat16)
            other = (1.0 - keep).astype(jnp.bfloat16)
            merged = own[part, :, j] * mine + mate_in[part, :, j] * other
            own[part, :, j] = merged

    def frame_copy(part, target, first=0, count=PAIRS):
        pairs = pl.ds(first, count)
        return pltpu.make_async_remote_copy(
            src_ref=own.at[part, target, pairs],
            dst_ref=recv.at[part, chip, pairs],
            send_sem=send_sem.at[part],
            recv_sem=recv_sem.at[part],
            device_id=(2 * target + core, det),
            device_id_type=MESH,
        )

    def ship(part, first=0, count=PAIRS, which=None):
        swap(part, first, count, which).wait_recv()
        merge(part, first, count)
        for step in STEPS:
            frame_copy(part, chip_at(step), first, count).start()

    def all_frames(part):
        chips = pl.ds(0, CHIPS - 1)
        return pltpu.make_async_remote_copy(
            src_ref=own.at[part, chips],
            dst_ref=recv.at[part, chips],
            send_sem=send_sem.at[part],
            recv_sem=recv_sem.at[part],
            device_id=(mate, det),
            device_id_type=MESH,
        )

    def join_copy():
        return pltpu.make_async_remote_copy(
            src_ref=fmate,
            dst_ref=fpart,
            send_sem=fswap_sem.at[0],
            recv_sem=fswap_sem.at[1],
            device_id=(mate, det),
            device_id_type=MESH,
        )

    places_of = ((col, lay), (lay, col))

    def ring_copy(half, d):
        mine = places_of[half][0]
        there = (mine + d) % RING
        target = lay * 4 + there if half == 0 else there * 4 + col
        return pltpu.make_async_remote_copy(
            src_ref=fsend.at[half, there],
            dst_ref=fring.at[half, mine],
            send_sem=fring_sem.at[half, 0],
            recv_sem=fring_sem.at[half, 1],
            device_id=(2 * target + core, det),
            device_id_type=MESH,
        )

    def last_copy(half, d):
        mine = places_of[half][1]
        there = (mine + d) % RING
        target = there * 4 + col if half == 0 else lay * 4 + there
        return pltpu.make_async_remote_copy(
            src_ref=fnext.at[half, there],
            dst_ref=flast.at[half, mine],
            send_sem=flast_sem.at[half, 0],
            recv_sem=flast_sem.at[half, 1],
            device_id=(2 * target + core, det),
            device_id_type=MESH,
        )

    def all_ring(half):
        others = pl.ds(0, RING - 1)
        return pltpu.make_async_remote_copy(
            src_ref=fsend.at[half, others],
            dst_ref=fring.at[half, others],
            send_sem=fring_sem.at[half, 0],
            recv_sem=fring_sem.at[half, 1],
            device_id=(mate, det),
            device_id_type=MESH,
        )

    def all_last(half):
        others = pl.ds(0, RING - 1)
        return pltpu.make_async_remote_copy(
            src_ref=fnext.at[half, others],
            dst_ref=flast.at[half, others],
            send_sem=flast_sem.at[half, 0],
            recv_sem=flast_sem.at[half, 1],
            device_id=(mate, det),
            device_id_type=MESH,
        )

    def code_fields():
        flat_copy.wait()
        dark_copy.wait()
        for half in range(HALVES):

            @pl.loop(0, HSEGS)
            def _(h, half=half):
                s = half * HSEGS + h
                mine = jnp.where(seg_owner[s] == proj, 1.0, 0.0)
                moved = []
                for ref, low, step in ((flat_v, 1.0, FLAT_STEP), (dark_v, 0.0, DARK_STEP)):
                    high, small = coded(stack_tiles(ref[s]), low, step)
                    both = jnp.dot(
                        pick[...],
                        jnp.concatenate([high, small], axis=1),
                        preferred_element_type=jnp.float32,
                    )
                    code = (both[:, :128] * 256.0 + both[:, 128:] - 32768.0) * mine
                    moved.append(code.reshape(PROJ, 8, 128))
                pair = jnp.concatenate(moved, axis=1).astype(jnp.int32).astype(jnp.int16)
                for z in range(RING):
                    for x in range(RING):
                        outer, inner = (x, z) if half == 0 else (z, x)
                        fsend[half, outer, inner, h] = pair[z * RING + x]
                        fmate[half, outer, inner, h] = pair[CHIPS + z * RING + x]

    def ship_fields():
        join_copy().wait()
        for half in range(HALVES):
            mine = places_of[half][0]

            @pl.loop(0, RING)
            def _(o, half=half):
                fsend[half, o] = (
                    fsend[half, o].astype(jnp.int32) + fpart[half, o].astype(jnp.int32)
                ).astype(jnp.int16)

            fring[half, mine] = fsend[half, mine]
        for d in (2, 1, 3):
            for half in range(HALVES):
                ring_copy(half, d).start()

    def pass_fields():
        for half in range(HALVES):
            all_ring(half).wait_recv()
            mine = places_of[half][1]

            @pl.loop(0, RING)
            def _(i, half=half):
                total = fring[half, 0, i].astype(jnp.int32)
                for o in range(1, RING):
                    total = total + fring[half, o, i].astype(jnp.int32)
                fnext[half, i] = total.astype(jnp.int16)

            flast[half, mine] = fnext[half, mine]
            for d in (2, 1, 3):
                last_copy(half, d).start()

    def take_fields():
        for half in range(HALVES):
            all_last(half).wait_recv()
            total = flast[half, 0].astype(jnp.int32)
            for i in range(1, RING):
                total = total + flast[half, i].astype(jnp.int32)
            code = (total + 32768).astype(jnp.float32)
            f = 1.0 + code[:, :8] * FLAT_STEP
            d = code[:, 8:] * DARK_STEP
            dark_s[half * HSEGS : (half + 1) * HSEGS] = d
            logflat_s[half * HSEGS : (half + 1) * HSEGS] = jnp.log(f - d)
            all_ring(half).wait_send()
            all_last(half).wait_send()

    def more(q):
        permute(q)
        swap(PARTS - 1 - q).start()

    for q in order[:2]:
        permute(q)
    pl.semaphore_wait(barrier, len(STEPS) + DET)
    for first, count, which in pieces:
        swap(0, first, count, which).start()
    swap(PARTS - 1).start()
    for first, count, which in pieces:
        ship(0, first, count, which)
    more(order[2])
    more(order[3])
    code_fields()
    join_copy().start()
    ship(1)
    ship_fields()
    more(order[4])
    more(order[5])
    ship(2)
    more(order[6])
    more(order[7])
    ship(3)
    pass_fields()
    for part in range(4, PARTS):
        ship(part)

    sub = lax.broadcasted_iota(jnp.int32, (8, 128), 0)
    lane = lax.broadcasted_iota(jnp.int32, (8, 128), 1)
    zero = jnp.zeros((8, 128), jnp.float32)

    def locate():
        lane16 = lax.broadcasted_iota(jnp.int32, (CHIPS, 128), 1)
        angle = angle_v[...]
        mirrored = angle
        for bit in (1, 2, 4, 8, 16, 32, 64):
            mirrored = jnp.where(
                lane16 & bit == 0, pltpu.roll(mirrored, 128 - bit, 1), pltpu.roll(mirrored, bit, 1)
            )
        angle = jnp.where(angle < ANGLES, angle, mirrored)
        angle = jnp.where(core == 0, angle, pltpu.roll(angle, SLOTS, 1))
        segment = segment_v[...]
        found = jnp.zeros((CHIPS, 128), jnp.int32)
        for s in range(1, SEGS):
            first = jnp.where(segment < s, 1, 0)
            for shift in (1, 2, 4):
                first = first + pltpu.roll(first, shift, 0)
            for shift in (1, 2, 4, 8, 16, 32, 64):
                first = first + pltpu.roll(first, shift, 1)
            found = found + jnp.where(angle >= jnp.concatenate([first, first], axis=0), 1, 0)
        segs_v[...] = found
        pltpu.make_async_copy(segs_v, segs, place_sem.at[0]).start()
        columns = jnp.transpose(angle)
        slots = [jnp.zeros((8, 128), jnp.int32)] * 8
        for c in range(CHIPS):
            for i in range(SLOTS // 8):
                column = jnp.broadcast_to(columns[8 * i : 8 * i + 8, c : c + 1], (8, 128)) - lane
                for b in range(8):
                    slots[b] = jnp.where(column == 128 * b, SLOTS * c + 8 * i + sub, slots[b])
        for b in range(8):
            best = slots[b]
            for shift in (1, 2, 4):
                best = jnp.maximum(best, pltpu.roll(best, shift, 0))
            places_v[b : b + 1, :] = best[:1]
        pltpu.make_async_copy(places_v, places, place_sem.at[1]).start()

    locate()
    take_fields()

    rim = ((sub < 2) & (lane < RIM)) | ((sub >= 6) & (lane >= 128 - RIM))

    pltpu.make_async_copy(segs_v, segs, place_sem.at[0]).wait()

    def absorb(part, accs):
        recv[part, chip] = own[part, chip]
        all_frames(part).wait()

        def batch(i, accs):
            accs = list(accs)
            for u in range(BATCH):
                source = BATCH * i + u
                outer = zero
                for j in range(PAIRS):
                    x = recv[part, source, j].astype(jnp.float32)
                    for f in range(2):
                        k = FRAMES * part + 2 * j + f
                        s = segs[source, k]
                        y = logflat_s[s] - jnp.log(x[8 * f : 8 * f + 8] - dark_s[s])
                        y = y.astype(jnp.bfloat16).astype(jnp.float32)
                        y_v[source * SLOTS + k] = y
                        accs[2 * (u % 2) + f] = accs[2 * (u % 2) + f] + y
                        outer = outer + pltpu.roll(jnp.where(rim, y, zero), 2 * RIM * (2 * j + f), 1)
                edges[part * CHIPS + source] = outer
            return tuple(accs)

        return lax.fori_loop(0, CHIPS // BATCH, batch, accs)

    accs = lax.fori_loop(0, PARTS, absorb, (zero,) * 4)
    for first, count, which in pieces:
        swap(0, first, count, which).wait_send()
    for part in range(1, PARTS):
        swap(part).wait_send()
    pltpu.make_async_copy(places_v, places, place_sem.at[1]).wait()
    profile = ((accs[0] + accs[1]) + (accs[2] + accs[3])) * (1.0 / ANGLES)

    def share(ref, which, t):
        return pltpu.make_async_remote_copy(
            src_ref=ref.at[det],
            dst_ref=ref.at[det],
            send_sem=small_sem.at[which, 0],
            recv_sem=small_sem.at[which, 1],
            device_id=(proj, (det + t) % DET),
            device_id_type=MESH,
        )

    def shared(ref, which):
        others = pl.ds(0, DET - 1)
        return pltpu.make_async_remote_copy(
            src_ref=ref.at[others],
            dst_ref=ref.at[others],
            send_sem=small_sem.at[which, 0],
            recv_sem=small_sem.at[which, 1],
            device_id=(mate, det),
            device_id_type=MESH,
        )

    def arrange(start, stop):
        @pl.loop(start, stop)
        def _(i):
            for u in range(16):
                ordered_out[i * 16 + u] = y_v[places[i // 8, 16 * (i % 8) + u]]

    profs[det] = profile
    for t in (1, 3, 2):
        share(profs, 0, t).start()
    low = jnp.where(sub < 2, zero, pltpu.roll(profile, 2, 0))
    high = jnp.where(sub >= 6, zero, pltpu.roll(profile, 6, 0))
    window = profile
    for o in range(1, RIM + 1):
        window = window + jnp.where(lane >= o, pltpu.roll(profile, o, 1), pltpu.roll(low, o, 1))
        window = window + jnp.where(
            lane < 128 - o, pltpu.roll(profile, 128 - o, 1), pltpu.roll(high, 128 - o, 1)
        )
    column = det * COLS_DEV + (sub // 2) * 128 + lane
    counted = jnp.minimum(column + RIM, COLS - 1) - jnp.maximum(column - RIM, 0) + 1
    counted = counted.astype(jnp.float32)
    inner = profile - window / counted

    def magnitude(i, accs):
        return tuple(
            accs[u] + jnp.abs(y_v[i * 16 + u] - inner) + jnp.abs(y_v[i * 16 + 8 + u] - inner)
            for u in range(8)
        )

    accs = lax.fori_loop(0, ANGLES // 16, magnitude, (zero,) * 8)
    total = ((accs[0] + accs[1]) + (accs[2] + accs[3])) + ((accs[4] + accs[5]) + (accs[6] + accs[7]))
    total = jnp.where(rim, zero, total)
    arrange(0, ARRANGED)
    shared(profs, 0).wait_recv()
    before = pltpu.roll(profs[(det + DET - 1) % DET], 2, 0)
    after = pltpu.roll(profs[(det + 1) % DET], 6, 0)
    before = jnp.where((sub < 2) & (det > 0), before, zero)
    after = jnp.where((sub >= 6) & (det < DET - 1), after, zero)
    for o in range(1, RIM + 1):
        window = window + jnp.where(lane < o, pltpu.roll(before, o, 1), zero)
        window = window + jnp.where(lane >= 128 - o, pltpu.roll(after, 128 - o, 1), zero)
    delta = profile - window / counted
    delta_out[...] = delta

    outer = zero
    for m in range(FRAMES):
        outer = outer + pltpu.roll(jnp.where(rim, delta, zero), 2 * RIM * m, 1)

    def rim_magnitude(i, accs):
        return tuple(accs[u] + jnp.abs(edges[i * 8 + u] - outer) for u in range(8))

    accs = lax.fori_loop(0, PARTS * CHIPS // 8, rim_magnitude, (total,) + (zero,) * 7)
    total = ((accs[0] + accs[1]) + (accs[2] + accs[3])) + ((accs[4] + accs[5]) + (accs[6] + accs[7]))
    sums[det] = total
    for t in (2, 1, 3):
        share(sums, 1, t).start()
    arrange(ARRANGED, ANGLES // 16)
    shared(sums, 1).wait_recv()
    total = (sums[0] + sums[1]) + (sums[2] + sums[3])
    rows = jnp.broadcast_to(jnp.sum(total, axis=1, keepdims=True), (8, 128))
    rows = rows + pltpu.roll(rows, 4, 0)
    rows = rows + pltpu.roll(rows, 2, 0)
    scale = rows * (1.0 / (ANGLES * COLS)) + EPSILON
    bins = jnp.where(
        sub % 2 == 0,
        bin_counts[row_order[2 * proj]],
        bin_counts[row_order[2 * proj + 1]],
    ).astype(jnp.float32)
    factor_out[...] = bins / scale

    for which, ref in enumerate((profs, sums)):
        shared(ref, which).wait_send()


BLOCK = 128
DEPTH = 4


def write_codes(ordered, delta, factor, out, block, sem):
    d, f = delta[...], factor[...]

    def copy(i):
        return pltpu.make_async_copy(
            block.at[i % DEPTH], out.at[pl.ds(i * BLOCK, BLOCK)], sem.at[i % DEPTH]
        )

    @pl.loop(0, ANGLES // BLOCK)
    def _(i):
        @pl.when(i >= DEPTH)
        def _():
            copy(i - DEPTH).wait()

        @pl.loop(0, BLOCK // 16)
        def _(k):
            for u in range(16):
                block[i % DEPTH, k * 16 + u] = (ordered[i * BLOCK + k * 16 + u] - d) * f

        copy(i).start()

    @pl.loop(ANGLES // BLOCK - DEPTH, ANGLES // BLOCK)
    def _(i):
        copy(i).wait()


def on_device(raw, slot_angle, segment_of, seg_owner, flat, dark, row_order, bin_counts):
    vmem = pl.BlockSpec(memory_space=pltpu.VMEM)
    hbm = pl.BlockSpec(memory_space=pltpu.HBM)
    dma = pltpu.SemaphoreType.DMA
    ordered, delta, factor = pl.pallas_call(
        exchange,
        name="exchange",
        out_shape=(
            jax.ShapeDtypeStruct((ANGLES, 8, 128), jnp.float32),
            jax.ShapeDtypeStruct((8, 128), jnp.float32),
            jax.ShapeDtypeStruct((8, 128), jnp.float32),
        ),
        in_specs=[hbm] * 8,
        out_specs=(vmem,) * 3,
        scratch_shapes=[
            pltpu.SMEM((CHIPS, 128), jnp.int32),
            pltpu.SMEM((SEGS,), jnp.int32),
            pltpu.SMEM((ROWS,), jnp.int32),
            pltpu.SMEM((ROWS,), jnp.int32),
            pltpu.VMEM((CHIPS, 128), jnp.int32),
            pltpu.VMEM((8, 128), jnp.int32),
            pltpu.SMEM((CHIPS, 128), jnp.int32),
            pltpu.VMEM((CHIPS, 128), jnp.int32),
            pltpu.SMEM((8, 128), jnp.int32),
            pltpu.VMEM((8, 128), jnp.int32),
            pltpu.VMEM((SLOTS, ROWS, COLS_DEV), jnp.bfloat16),
            pltpu.VMEM((PARTS, CHIPS, PAIRS, 16, 128), jnp.bfloat16),
            pltpu.VMEM((PARTS, CHIPS, PAIRS, 16, 128), jnp.bfloat16),
            pltpu.VMEM((PARTS, CHIPS, PAIRS, 16, 128), jnp.bfloat16),
            pltpu.VMEM((PARTS, CHIPS, PAIRS, 16, 128), jnp.bfloat16),
            pltpu.VMEM((ANGLES, 8, 128), jnp.float32),
            pltpu.VMEM((SEGS, ROWS, COLS_DEV), jnp.float32),
            pltpu.VMEM((SEGS, ROWS, COLS_DEV), jnp.float32),
            pltpu.VMEM((256, 256), jnp.float32),
            pltpu.VMEM((256, 256), jnp.bfloat16),
            pltpu.VMEM((HALVES, RING, RING, HSEGS, 16, 128), jnp.int16),
            pltpu.VMEM((HALVES, RING, RING, HSEGS, 16, 128), jnp.int16),
            pltpu.VMEM((HALVES, RING, RING, HSEGS, 16, 128), jnp.int16),
            pltpu.VMEM((HALVES, RING, RING, HSEGS, 16, 128), jnp.int16),
            pltpu.VMEM((HALVES, RING, HSEGS, 16, 128), jnp.int16),
            pltpu.VMEM((HALVES, RING, HSEGS, 16, 128), jnp.int16),
            pltpu.VMEM((PARTS * CHIPS, 8, 128), jnp.float32),
            pltpu.VMEM((SEGS, 8, 128), jnp.float32),
            pltpu.VMEM((SEGS, 8, 128), jnp.float32),
            pltpu.VMEM((DET, 8, 128), jnp.float32),
            pltpu.VMEM((DET, 8, 128), jnp.float32),
            dma((6,)),
            dma((PARTS,)),
            dma((2,)),
            dma((2,)),
            dma((PARTS + 1,)),
            dma((PARTS + 1,)),
            dma((PARTS,)),
            dma((PARTS,)),
            dma((2,)),
            dma((HALVES, 2)),
            dma((HALVES, 2)),
            dma((2, 2)),
        ],
        compiler_params=pltpu.CompilerParams(
            collective_id=0, has_side_effects=True, vmem_limit_bytes=40 << 20
        ),
    )(
        *(
            pltpu.with_memory_space_constraint(a, pltpu.HBM)
            for a in (
                slot_angle.reshape(CHIPS, 2 * SLOTS),
                segment_of.reshape(8, 128),
                seg_owner,
                row_order,
                bin_counts,
                raw,
                flat,
                dark,
            )
        )
    )
    codes = pl.pallas_call(
        write_codes,
        name="write_codes",
        out_shape=jax.ShapeDtypeStruct((ANGLES, 8, 128), jnp.float32),
        in_specs=[vmem, vmem, vmem],
        out_specs=hbm,
        scratch_shapes=[pltpu.VMEM((DEPTH, BLOCK, 8, 128), jnp.float32), dma((DEPTH,))],
        compiler_params=pltpu.CompilerParams(vmem_limit_bytes=16 << 20),
    )(ordered, delta, factor)
    return codes.reshape(ANGLES, TILES, 2, 128).transpose(0, 2, 1, 3).reshape(ANGLES, 2, COLS_DEV)


def solution(mesh):
    return jax.shard_map(
        on_device,
        mesh=mesh,
        in_specs=(
            P("proj", None, "det"),
            P(),
            P(),
            P(),
            P("proj", None, "det"),
            P("proj", None, "det"),
            P(),
            P(),
        ),
        out_specs=P(None, "proj", "det"),
        check_vma=False,
    )
```

time: 55.5 us -> 50.1 us (0.903)
  Pallas kernels: 55.3 us -> 50 us
    pallas_call x1, Pallas kernels: 53 us -> 47.6 us  [on_device(): pl.pallas_call(exchange, name='exchange', out_shape=(jax.ShapeDtypeStruct...]
where the time goes in v3:
time: 50.1 us; the launch traced here: 50 us
  Pallas kernels  50 us (100%)
    pallas_call x1, Pallas kernels, on_device(): pl.pallas_call(exchange, name='exchange', out_shape=(jax.ShapeDtypeStruct...  47.6 us
    pallas_call x1, Pallas kernels, on_device(): pl.pallas_call(write_codes, name='write_codes', out_shape=jax.ShapeDtypeS...  2.32 us

profile of v3, /device:TPU:0, one launch (start us, length us, event | category | flops | bytes accessed | tf_op | source)
XLA Modules:
  0.0 50.0 jit_solution(7734078137244596119)
XLA Ops:
  0.0 47.6 %exchange.1 = (f32[1024,8,128]{2,1,0:T(8,128)S(1)}, f32[8,128]{1,0:T(8,128)S(1)}, f32[8,128]{1,0:T(8,128)S(1)}) custom-call(s32[16,128]{1,0:T(8,128)} %bitcast.7, s32[8,128]{1,0:T(8,128)} %bitcast.8, s32[8]{0:T(128)} %seg_owner_h.1, s32[64]{0:T(128)} %row_order_h.1, s32[64]{0:T(128)} %bin_counts_h.1, bf16[64,64,512]{2,1,0:T(8,128)(2,1)} %raw.1, ...), custom_call_target="tpu_custom_call" | custom-call | tf_op jit(solution)/shard_map/exchange/pallas_call | solution.py:610
  47.6 2.3 %write_codes.1 = f32[1024,8,128]{2,1,0:T(8,128)} custom-call(f32[1024,8,128]{2,1,0:T(8,128)S(1)} %get-tuple-element.8.ordered, f32[8,128]{1,0:T(8,128)S(1)} %get-tuple-element.9.delta, f32[8,128]{1,0:T(8,128)S(1)} %get-tuple-element.10.factor), custom_call_target="tpu_custom_call" | custom-call | tf_op jit(solution)/shard_map/write_codes/pallas_call | solution.py:683

commit v4 on v3

--- a/solution.py
+++ b/solution.py
@@ -22,7 +22,7 @@
 FRAMES = SLOTS // PARTS
 PAIRS = FRAMES // 2
 HEAD = 1
-BATCH = 4
+BATCH = 8
 ARRANGED = 20
 HALVES = 2
 RING = 4
@@ -143,11 +143,11 @@
     for q in order:
         block = pl.ds(FRAMES * q, FRAMES)
         loads[q] = pltpu.make_async_copy(raw.at[block], frames.at[block], load_sem.at[q])
-        loads[q].start()
     flat_copy = pltpu.make_async_copy(flat, flat_v, field_sem.at[0])
     dark_copy = pltpu.make_async_copy(dark, dark_v, field_sem.at[1])
-    flat_copy.start()
-    dark_copy.start()
+
+    for q in order[:2]:
+        loads[q].start()
 
     for copy in ints:
         copy.wait()
@@ -379,6 +379,12 @@
 
     for q in order[:2]:
         permute(q)
+    for q in order[2:4]:
+        loads[q].start()
+    flat_copy.start()
+    dark_copy.start()
+    for q in order[4:]:
+        loads[q].start()
     pl.semaphore_wait(barrier, len(STEPS) + DET)
     for first, count, which in pieces:
         swap(0, first, count, which).start()
@@ -446,6 +452,11 @@
     rim = ((sub < 2) & (lane < RIM)) | ((sub >= 6) & (lane >= 128 - RIM))
 
     pltpu.make_async_copy(segs_v, segs, place_sem.at[0]).wait()
+    for first, count, which in pieces:
+        swap(0, first, count, which).wait_send()
+    for part in range(1, PARTS):
+        swap(part).wait_send()
+    pltpu.make_async_copy(places_v, places, place_sem.at[1]).wait()
 
     def absorb(part, accs):
         recv[part, chip] = own[part, chip]
@@ -472,11 +483,6 @@
         return lax.fori_loop(0, CHIPS // BATCH, batch, accs)
 
     accs = lax.fori_loop(0, PARTS, absorb, (zero,) * 4)
-    for first, count, which in pieces:
-        swap(0, first, count, which).wait_send()
-    for part in range(1, PARTS):
-        swap(part).wait_send()
-    pltpu.make_async_copy(places_v, places, place_sem.at[1]).wait()
     profile = ((accs[0] + accs[1]) + (accs[2] + accs[3])) * (1.0 / ANGLES)
 
     def share(ref, which, t):
@@ -489,8 +495,8 @@
             device_id_type=MESH,
         )
 
-    def shared(ref, which):
-        others = pl.ds(0, DET - 1)
+    def shared(ref, which, count):
+        others = pl.ds(0, count)
         return pltpu.make_async_remote_copy(
             src_ref=ref.at[others],
             dst_ref=ref.at[others],
@@ -507,7 +513,7 @@
                 ordered_out[i * 16 + u] = y_v[places[i // 8, 16 * (i % 8) + u]]
 
     profs[det] = profile
-    for t in (1, 3, 2):
+    for t in (1, 3):
         share(profs, 0, t).start()
     low = jnp.where(sub < 2, zero, pltpu.roll(profile, 2, 0))
     high = jnp.where(sub >= 6, zero, pltpu.roll(profile, 6, 0))
@@ -532,7 +538,7 @@
     total = ((accs[0] + accs[1]) + (accs[2] + accs[3])) + ((accs[4] + accs[5]) + (accs[6] + accs[7]))
     total = jnp.where(rim, zero, total)
     arrange(0, ARRANGED)
-    shared(profs, 0).wait_recv()
+    shared(profs, 0, 2).wait_recv()
     before = pltpu.roll(profs[(det + DET - 1) % DET], 2, 0)
     after = pltpu.roll(profs[(det + 1) % DET], 6, 0)
     before = jnp.where((sub < 2) & (det > 0), before, zero)
@@ -556,7 +562,7 @@
     for t in (2, 1, 3):
         share(sums, 1, t).start()
     arrange(ARRANGED, ANGLES // 16)
-    shared(sums, 1).wait_recv()
+    shared(sums, 1, DET - 1).wait_recv()
     total = (sums[0] + sums[1]) + (sums[2] + sums[3])
     rows = jnp.broadcast_to(jnp.sum(total, axis=1, keepdims=True), (8, 128))
     rows = rows + pltpu.roll(rows, 4, 0)
@@ -569,12 +575,12 @@
     ).astype(jnp.float32)
     factor_out[...] = bins / scale
 
-    for which, ref in enumerate((profs, sums)):
-        shared(ref, which).wait_send()
-
-
-BLOCK = 128
-DEPTH = 4
+    shared(profs, 0, 2).wait_send()
+    shared(sums, 1, DET - 1).wait_send()
+
+
+BLOCK = 64
+DEPTH = 16
 
 
 def write_codes(ordered, delta, factor, out, block, sem):

time: 50.1 us -> 48.6 us (0.970)
  Pallas kernels: 50 us -> 48.5 us
    pallas_call x1, Pallas kernels: 47.6 us -> 46.3 us  [on_device(): pl.pallas_call(exchange, name='exchange', out_shape=(jax.ShapeDtypeStruct...]
where the time goes in v4:
time: 48.6 us; the launch traced here: 48.5 us
  Pallas kernels  48.5 us (100%)
    pallas_call x1, Pallas kernels, on_device(): pl.pallas_call(exchange, name='exchange', out_shape=(jax.ShapeDtypeStruct...  46.3 us
    pallas_call x1, Pallas kernels, on_device(): pl.pallas_call(write_codes, name='write_codes', out_shape=jax.ShapeDtypeS...  2.19 us

profile of v4, /device:TPU:0, one launch (start us, length us, event | category | flops | bytes accessed | tf_op | source)
XLA Modules:
  0.0 48.5 jit_solution(4152307802851079154)
XLA Ops:
  0.0 46.3 %exchange.1 = (f32[1024,8,128]{2,1,0:T(8,128)S(1)}, f32[8,128]{1,0:T(8,128)S(1)}, f32[8,128]{1,0:T(8,128)S(1)}) custom-call(s32[16,128]{1,0:T(8,128)} %bitcast.7, s32[8,128]{1,0:T(8,128)} %bitcast.8, s32[8]{0:T(128)} %seg_owner_h.1, s32[64]{0:T(128)} %row_order_h.1, s32[64]{0:T(128)} %bin_counts_h.1, bf16[64,64,512]{2,1,0:T(8,128)(2,1)} %raw.1, ...), custom_call_target="tpu_custom_call" | custom-call | tf_op jit(solution)/shard_map/exchange/pallas_call | solution.py:616
  46.3 2.2 %write_codes.1 = f32[1024,8,128]{2,1,0:T(8,128)} custom-call(f32[1024,8,128]{2,1,0:T(8,128)S(1)} %get-tuple-element.8.ordered, f32[8,128]{1,0:T(8,128)S(1)} %get-tuple-element.9.delta, f32[8,128]{1,0:T(8,128)S(1)} %get-tuple-element.10.factor), custom_call_target="tpu_custom_call" | custom-call | tf_op jit(solution)/shard_map/write_codes/pallas_call | solution.py:689

commit v5 on v4

--- a/solution.py
+++ b/solution.py
@@ -22,6 +22,7 @@
 FRAMES = SLOTS // PARTS
 PAIRS = FRAMES // 2
 HEAD = 1
+LAST = ((0, 7), (7, 15))
 BATCH = 8
 ARRANGED = 20
 HALVES = 2
@@ -189,7 +190,7 @@
         return pltpu.make_async_remote_copy(
             src_ref=away.at[part, :, pairs],
             dst_ref=mate_in.at[part, :, pairs],
-            send_sem=swap_ssem.at[which],
+            send_sem=swap_ssem.at[0],
             recv_sem=swap_rsem.at[which],
             device_id=(mate, det),
             device_id_type=MESH,
@@ -213,16 +214,24 @@
             merged = own[part, :, j] * mine + mate_in[part, :, j] * other
             own[part, :, j] = merged
 
-    def frame_copy(part, target, first=0, count=PAIRS):
+    def frame_copy(part, target, first=0, count=PAIRS, sem=None):
         pairs = pl.ds(first, count)
         return pltpu.make_async_remote_copy(
             src_ref=own.at[part, target, pairs],
             dst_ref=recv.at[part, chip, pairs],
-            send_sem=send_sem.at[part],
-            recv_sem=recv_sem.at[part],
+            send_sem=send_sem.at[0],
+            recv_sem=recv_sem.at[part if sem is None else sem],
             device_id=(2 * target + core, det),
             device_id_type=MESH,
         )
+
+    def ship_last():
+        part = PARTS - 1
+        swap(part).wait_recv()
+        merge(part)
+        for i, (first, stop) in enumerate(LAST):
+            for step in STEPS[first:stop]:
+                frame_copy(part, chip_at(step), sem=part + i).start()
 
     def ship(part, first=0, count=PAIRS, which=None):
         swap(part, first, count, which).wait_recv()
@@ -230,12 +239,23 @@
         for step in STEPS:
             frame_copy(part, chip_at(step), first, count).start()
 
+    def last_frames(i):
+        chips = pl.ds(0, LAST[i][1] - LAST[i][0])
+        return pltpu.make_async_remote_copy(
+            src_ref=own.at[PARTS - 1, chips],
+            dst_ref=recv.at[PARTS - 1, chips],
+            send_sem=send_sem.at[0],
+            recv_sem=recv_sem.at[PARTS - 1 + i],
+            device_id=(mate, det),
+            device_id_type=MESH,
+        )
+
     def all_frames(part):
         chips = pl.ds(0, CHIPS - 1)
         return pltpu.make_async_remote_copy(
             src_ref=own.at[part, chips],
             dst_ref=recv.at[part, chips],
-            send_sem=send_sem.at[part],
+            send_sem=send_sem.at[0],
             recv_sem=recv_sem.at[part],
             device_id=(mate, det),
             device_id_type=MESH,
@@ -310,16 +330,17 @@
             def _(h, half=half):
                 s = half * HSEGS + h
                 mine = jnp.where(seg_owner[s] == proj, 1.0, 0.0)
+                parts = [
+                    *coded(stack_tiles(flat_v[s]), 1.0, FLAT_STEP),
+                    *coded(stack_tiles(dark_v[s]), 0.0, DARK_STEP),
+                ]
+                both = jnp.dot(
+                    pick[...], jnp.concatenate(parts, axis=1), preferred_element_type=jnp.float32
+                )
                 moved = []
-                for ref, low, step in ((flat_v, 1.0, FLAT_STEP), (dark_v, 0.0, DARK_STEP)):
-                    high, small = coded(stack_tiles(ref[s]), low, step)
-                    both = jnp.dot(
-                        pick[...],
-                        jnp.concatenate([high, small], axis=1),
-                        preferred_element_type=jnp.float32,
-                    )
-                    code = (both[:, :128] * 256.0 + both[:, 128:] - 32768.0) * mine
-                    moved.append(code.reshape(PROJ, 8, 128))
+                for i in (0, 256):
+                    code = both[:, i : i + 128] * 256.0 + both[:, i + 128 : i + 256] - 32768.0
+                    moved.append((code * mine).reshape(PROJ, 8, 128))
                 pair = jnp.concatenate(moved, axis=1).astype(jnp.int32).astype(jnp.int16)
                 for z in range(RING):
                     for x in range(RING):
@@ -396,16 +417,17 @@
     code_fields()
     join_copy().start()
     ship(1)
+    more(order[4])
     ship_fields()
-    more(order[4])
     more(order[5])
     ship(2)
     more(order[6])
     more(order[7])
     ship(3)
     pass_fields()
-    for part in range(4, PARTS):
+    for part in range(4, PARTS - 1):
         ship(part)
+    ship_last()
 
     sub = lax.broadcasted_iota(jnp.int32, (8, 128), 0)
     lane = lax.broadcasted_iota(jnp.int32, (8, 128), 1)
@@ -452,37 +474,48 @@
     rim = ((sub < 2) & (lane < RIM)) | ((sub >= 6) & (lane >= 128 - RIM))
 
     pltpu.make_async_copy(segs_v, segs, place_sem.at[0]).wait()
-    for first, count, which in pieces:
-        swap(0, first, count, which).wait_send()
-    for part in range(1, PARTS):
-        swap(part).wait_send()
+    pltpu.make_async_remote_copy(
+        src_ref=away,
+        dst_ref=mate_in,
+        send_sem=swap_ssem.at[0],
+        recv_sem=swap_rsem.at[0],
+        device_id=(mate, det),
+        device_id_type=MESH,
+    ).wait_send()
     pltpu.make_async_copy(places_v, places, place_sem.at[1]).wait()
+
+    def absorb_from(part, sources, accs):
+        accs = list(accs)
+        for u, source in enumerate(sources):
+            outer = zero
+            for j in range(PAIRS):
+                x = recv[part, source, j].astype(jnp.float32)
+                for f in range(2):
+                    k = FRAMES * part + 2 * j + f
+                    s = segs[source, k]
+                    y = logflat_s[s] - jnp.log(x[8 * f : 8 * f + 8] - dark_s[s])
+                    y = y.astype(jnp.bfloat16).astype(jnp.float32)
+                    y_v[source * SLOTS + k] = y
+                    accs[2 * (u % 2) + f] = accs[2 * (u % 2) + f] + y
+                    outer = outer + pltpu.roll(jnp.where(rim, y, zero), 2 * RIM * (2 * j + f), 1)
+            edges[part * CHIPS + source] = outer
+        return tuple(accs)
 
     def absorb(part, accs):
         recv[part, chip] = own[part, chip]
-        all_frames(part).wait()
+        all_frames(part).wait_recv()
 
         def batch(i, accs):
-            accs = list(accs)
-            for u in range(BATCH):
-                source = BATCH * i + u
-                outer = zero
-                for j in range(PAIRS):
-                    x = recv[part, source, j].astype(jnp.float32)
-                    for f in range(2):
-                        k = FRAMES * part + 2 * j + f
-                        s = segs[source, k]
-                        y = logflat_s[s] - jnp.log(x[8 * f : 8 * f + 8] - dark_s[s])
-                        y = y.astype(jnp.bfloat16).astype(jnp.float32)
-                        y_v[source * SLOTS + k] = y
-                        accs[2 * (u % 2) + f] = accs[2 * (u % 2) + f] + y
-                        outer = outer + pltpu.roll(jnp.where(rim, y, zero), 2 * RIM * (2 * j + f), 1)
-                edges[part * CHIPS + source] = outer
-            return tuple(accs)
+            return absorb_from(part, [BATCH * i + u for u in range(BATCH)], accs)
 
         return lax.fori_loop(0, CHIPS // BATCH, batch, accs)
 
-    accs = lax.fori_loop(0, PARTS, absorb, (zero,) * 4)
+    accs = lax.fori_loop(0, PARTS - 1, absorb, (zero,) * 4)
+    recv[PARTS - 1, chip] = own[PARTS - 1, chip]
+    for i, (first, stop) in enumerate(LAST):
+        last_frames(i).wait_recv()
+        sources = [chip_at((4 - step[0], 4 - step[1])) for step in STEPS[first:stop]]
+        accs = absorb_from(PARTS - 1, sources + ([chip] if i == 0 else []), accs)
     profile = ((accs[0] + accs[1]) + (accs[2] + accs[3])) * (1.0 / ANGLES)
 
     def share(ref, which, t):
@@ -575,6 +608,15 @@
     ).astype(jnp.float32)
     factor_out[...] = bins / scale
 
+    every = (pl.ds(0, PARTS), pl.ds(0, CHIPS - 1))
+    pltpu.make_async_remote_copy(
+        src_ref=own.at[every],
+        dst_ref=recv.at[every],
+        send_sem=send_sem.at[0],
+        recv_sem=recv_sem.at[0],
+        device_id=(mate, det),
+        device_id_type=MESH,
+    ).wait_send()
     shared(profs, 0, 2).wait_send()
     shared(sums, 1, DET - 1).wait_send()
 
@@ -659,10 +701,10 @@
             dma((PARTS,)),
             dma((2,)),
             dma((2,)),
+            dma((1,)),
             dma((PARTS + 1,)),
-            dma((PARTS + 1,)),
-            dma((PARTS,)),
-            dma((PARTS,)),
+            dma((1,)),
+            dma((PARTS - 1 + len(LAST),)),
             dma((2,)),
             dma((HALVES, 2)),
             dma((HALVES, 2)),

time: 48.6 us -> 48.4 us (level)
  no operation moved by 1% of the time
where the time goes in v5:
time: 48.4 us; the launch traced here: 48.3 us
  Pallas kernels  48.3 us (100%)
    pallas_call x1, Pallas kernels, on_device(): pl.pallas_call(exchange, name='exchange', out_shape=(jax.ShapeDtypeStruct...  46.1 us
    pallas_call x1, Pallas kernels, on_device(): pl.pallas_call(write_codes, name='write_codes', out_shape=jax.ShapeDtypeS...  2.19 us

profile of v5, /device:TPU:0, one launch (start us, length us, event | category | flops | bytes accessed | tf_op | source)
XLA Modules:
  0.0 48.3 jit_solution(4506786929825702979)
XLA Ops:
  0.0 46.1 %exchange.1 = (f32[1024,8,128]{2,1,0:T(8,128)S(1)}, f32[8,128]{1,0:T(8,128)S(1)}, f32[8,128]{1,0:T(8,128)S(1)}) custom-call(s32[16,128]{1,0:T(8,128)} %bitcast.7, s32[8,128]{1,0:T(8,128)} %bitcast.8, s32[8]{0:T(128)} %seg_owner_h.1, s32[64]{0:T(128)} %row_order_h.1, s32[64]{0:T(128)} %bin_counts_h.1, bf16[64,64,512]{2,1,0:T(8,128)(2,1)} %raw.1, ...), custom_call_target="tpu_custom_call" | custom-call | tf_op jit(solution)/shard_map/exchange/pallas_call | solution.py:658
  46.1 2.2 %write_codes.1 = f32[1024,8,128]{2,1,0:T(8,128)} custom-call(f32[1024,8,128]{2,1,0:T(8,128)S(1)} %get-tuple-element.8.ordered, f32[8,128]{1,0:T(8,128)S(1)} %get-tuple-element.9.delta, f32[8,128]{1,0:T(8,128)S(1)} %get-tuple-element.10.factor), custom_call_target="tpu_custom_call" | custom-call | tf_op jit(solution)/shard_map/write_codes/pallas_call | solution.py:731

commit v6 on v5

--- a/solution.py
+++ b/solution.py
@@ -409,18 +409,19 @@
     pl.semaphore_wait(barrier, len(STEPS) + DET)
     for first, count, which in pieces:
         swap(0, first, count, which).start()
-    swap(PARTS - 1).start()
     for first, count, which in pieces:
         ship(0, first, count, which)
     more(order[2])
-    more(order[3])
+    permute(order[3])
     code_fields()
     join_copy().start()
     ship(1)
     more(order[4])
     ship_fields()
-    more(order[5])
+    permute(order[5])
     ship(2)
+    for q in (order[1], order[3], order[5]):
+        swap(PARTS - 1 - q).start()
     more(order[6])
     more(order[7])
     ship(3)

time: 48.4 us -> 48.4 us (level)
  no operation moved by 1% of the time
where the time goes in v6:
time: 48.4 us; the launch traced here: 48.3 us
  Pallas kernels  48.3 us (100%)
    pallas_call x1, Pallas kernels, on_device(): pl.pallas_call(exchange, name='exchange', out_shape=(jax.ShapeDtypeStruct...  46.1 us
    pallas_call x1, Pallas kernels, on_device(): pl.pallas_call(write_codes, name='write_codes', out_shape=jax.ShapeDtypeS...  2.19 us

profile of v6, /device:TPU:0, one launch (start us, length us, event | category | flops | bytes accessed | tf_op | source)
XLA Modules:
  0.0 48.3 jit_solution(8118221554740815432)
XLA Ops:
  0.0 46.1 %exchange.1 = (f32[1024,8,128]{2,1,0:T(8,128)S(1)}, f32[8,128]{1,0:T(8,128)S(1)}, f32[8,128]{1,0:T(8,128)S(1)}) custom-call(s32[16,128]{1,0:T(8,128)} %bitcast.7, s32[8,128]{1,0:T(8,128)} %bitcast.8, s32[8]{0:T(128)} %seg_owner_h.1, s32[64]{0:T(128)} %row_order_h.1, s32[64]{0:T(128)} %bin_counts_h.1, bf16[64,64,512]{2,1,0:T(8,128)(2,1)} %raw.1, ...), custom_call_target="tpu_custom_call" | custom-call | tf_op jit(solution)/shard_map/exchange/pallas_call | solution.py:659
  46.1 2.2 %write_codes.1 = f32[1024,8,128]{2,1,0:T(8,128)} custom-call(f32[1024,8,128]{2,1,0:T(8,128)S(1)} %get-tuple-element.8.ordered, f32[8,128]{1,0:T(8,128)S(1)} %get-tuple-element.9.delta, f32[8,128]{1,0:T(8,128)S(1)} %get-tuple-element.10.factor), custom_call_target="tpu_custom_call" | custom-call | tf_op jit(solution)/shard_map/write_codes/pallas_call | solution.py:732
